TPU v7x, 32 devices: a whole 2x2x4 slice. The times are simulated.
32 devices in a mesh: lat: 4 (over z), lon: 8 (over y, x, core).
Axes of the slice: x: 2, y: 2, z: 4, core: 2. Of those that a mesh axis runs over, the one named last changes fastest.
Arguments:
- east_courant: float32 [2, 16, 384, 1024], P(None, None, 'lat', 'lon'), may hold values from 0.3 to 400
- north_courant: float32 [2, 16, 384, 1024], P(None, None, 'lat', 'lon'), may hold values from -0.45 to 0.45
- kernels: float32 [2, 16, 8192], P(None, None, ('lat', 'lon')), may hold values from 0.1 to 1.2
- departures: float32 [2, 2, 8192], P(None, None, ('lat', 'lon')), may hold values from -6 to 6
- cells: int32 [2, 8192], P(None, ('lat', 'lon')), may hold values from 0 to 12287
- counts: int32 [2, 1024], P(None, ('lat', 'lon')), may hold values from 1 to 8, as said below
Outputs:
- adjoint_state: float32 [2, 16, 384, 1024], P(None, None, 'lat', 'lon')
- flux_gradient: float32 [2, 384, 1024], P(None, 'lat', 'lon')
Inputs may be any that keep to these rules, and one draw needn't show every extreme that they name: counts[n, s * 32 + o] is the number of live slots from device s to owner o in step n; in every step some owner receives 8 from every device. `cells`: a cell of the owner's block, row-major over 96 x 128.
All inputs are finite; a program needn't handle non-finite values.
Results may differ from a plain program's by a relative error of at most 0.0003.
Values sent between devices are 32-bit elements; how exact they have to be, the bound alone decides.
A program may use at most 192 MiB of HBM per device.

v0:
```python
import math

import jax
import jax.numpy as jnp
from jax import lax
from jax.sharding import PartitionSpec as P


def with_halo(shard, sides, width):
    for axis, dim in sides:
        size, length = (lax.axis_size(axis), shard.shape[dim])
        up = [(i, (i + 1) % size) for i in range(size - 1)]
        down = [(j, i) for i, j in up]
        last = lax.slice_in_dim(shard, length - width, length, axis=dim)
        leading = lax.slice_in_dim(shard, 0, width, axis=dim)
        before = lax.ppermute(last, axis, up)
        after = lax.ppermute(leading, axis, down)
        shard = jnp.concatenate([before, shard, after], axis=dim)
    return shard


def compose(outer_map, inner_map):
    return (outer_map[0] * inner_map[0], outer_map[0] * inner_map[1] + outer_map[1])


def reverse_pair(higher, lower_map):
    return compose(lower_map, higher)


def suffix_maps(retain, source):
    return lax.associative_scan(reverse_pair, (retain, source), reverse=True, axis=source.ndim - 1)


def deposit(terms, slot_cells, cell_total):
    block_cells = math.gcd(cell_total, 2048)
    block_count = cell_total // block_cells

    def one_block(block_start):
        places = block_start + lax.broadcasted_iota(
            jnp.int32, (slot_cells.shape[0], block_cells), 1
        )
        onehot = (slot_cells[:, None] == places).astype(jnp.float32)
        return jnp.dot(
            terms, onehot, precision=lax.Precision.HIGHEST, preferred_element_type=jnp.float32
        )

    starts = jnp.arange(block_count, dtype=jnp.int32) * block_cells
    pieces = lax.map(one_block, starts)
    return jnp.swapaxes(pieces, 0, 1).reshape(terms.shape[0], cell_total)


def lat_adjoint(adjoint, north, is_top):
    tracers = adjoint.shape[0]
    lat_rows = north.shape[1]
    top_row = (lax.broadcasted_iota(jnp.int32, north.shape, 1) == lat_rows - 1) & is_top
    north_faces = jnp.where(top_row, 0.0, north)
    northward = jnp.maximum(north_faces, 0.0)
    southward = jnp.minimum(north_faces, 0.0)
    stacked = jnp.concatenate([adjoint, southward[None]], 0)
    padded = with_halo(stacked, (("lat", 2),), 1)
    upper_row = padded[:tracers, :, 2:]
    lower_row = padded[:tracers, :, :-2]
    south_faces = padded[tracers:, :, :-2]
    return adjoint + northward * (upper_row - adjoint) + south_faces * (adjoint - lower_row)


def pencil_solve(adjoint, east_pencil):
    tracers, levels, lat_rows, lon_cells = adjoint.shape
    retain = east_pencil / (1.0 + east_pencil)
    weight = 1.0 / (1.0 + east_pencil)
    pencil = lax.all_to_all(
        adjoint.reshape(tracers, levels * lat_rows, lon_cells),
        "lon",
        split_axis=1,
        concat_axis=2,
        tiled=True,
    )
    gains, rests = suffix_maps(jnp.broadcast_to(retain, pencil.shape), weight * pencil)
    closure = rests[:, :, :1] / (1.0 - gains[:, :, :1])
    solved = gains * closure + rests
    moved = lax.all_to_all(solved, "lon", split_axis=2, concat_axis=1, tiled=True)
    return moved.reshape(adjoint.shape)


def shards(east_courant, north_courant, kernels, departures, cells, counts):
    steps_total, levels, lat_rows, lon_cells = east_courant.shape
    tracers = departures.shape[1]
    owners = counts.shape[1]
    slot_count = cells.shape[1]
    capacity = slot_count // owners
    within = lax.broadcasted_iota(jnp.int32, (steps_total, owners, capacity), 2)
    live_slot = (within < counts[:, :, None]).reshape(steps_total, slot_count)
    values = departures * live_slot[:, None, :].astype(jnp.float32)
    places = cells.astype(jnp.float32)[:, None, :]
    arrived = (
        lax.all_to_all(kernels, ("lat", "lon"), split_axis=2, concat_axis=2, tiled=True),
        lax.all_to_all(values, ("lat", "lon"), split_axis=2, concat_axis=2, tiled=True),
        lax.all_to_all(places, ("lat", "lon"), split_axis=2, concat_axis=2, tiled=True),
    )
    got_kernels, got_values, got_places = arrived
    got_cells = got_places[:, 0, :].astype(jnp.int32)
    is_top = lax.axis_index("lat") == lax.axis_size("lat") - 1
    east_rows = east_courant.reshape(steps_total, levels * lat_rows, lon_cells)
    east_pencils = lax.all_to_all(east_rows, "lon", split_axis=1, concat_axis=2, tiled=True)
    adjoint = jnp.zeros((tracers, levels, lat_rows, lon_cells), jnp.float32)
    flux_gradient = jnp.zeros((tracers, lat_rows, lon_cells), jnp.float32)
    for window_step in range(steps_total - 1, -1, -1):
        terms = got_values[window_step][:, None, :] * got_kernels[window_step][None, :, :]
        flat_terms = terms.reshape(tracers * levels, terms.shape[-1])
        added = deposit(flat_terms, got_cells[window_step], lat_rows * lon_cells)
        adjoint = adjoint + added.reshape(adjoint.shape)
        flux_gradient = flux_gradient + adjoint[:, 0]
        adjoint = lat_adjoint(adjoint, north_courant[window_step], is_top)
        adjoint = pencil_solve(adjoint, east_pencils[window_step])
    return (adjoint, flux_gradient)


def solution(mesh):
    return jax.shard_map(
        shards,
        mesh=mesh,
        in_specs=(
            P(None, None, "lat", "lon"),
            P(None, None, "lat", "lon"),
            P(None, None, ("lat", "lon")),
            P(None, None, ("lat", "lon")),
            P(None, ("lat", "lon")),
            P(None, ("lat", "lon")),
        ),
        out_specs=(P(None, None, "lat", "lon"), P(None, "lat", "lon")),
        check_vma=False,
    )
```

profile of v0, /device:TPU:0, one launch (start us, length us, event | category | flops | bytes accessed | tf_op | source)
XLA Modules:
  0.0 1813.9 jit_solution(8451227947129288689)
XLA Ops:
  96.4 16.8 slice.785
  113.2 16.8 slice.787
  130.0 16.3 slice.783
  181.8 32.0 %slice.845 = f32[2,192,512]{2,1,0:T(8,128)} slice(f32[2,192,1024]{2,1,0:T(8,128)S(1)} %bitcast_multiply_fusion.1), slice={[0:2:1], [0:192:1], [0:1023:2]} | slice | bytes 1572864 | tf_op jit(solution)/shard_map/slice | solution.py:31
  213.7 31.5 %slice.843 = f32[2,192,512]{2,1,0:T(8,128)} slice(f32[2,192,1024]{2,1,0:T(8,128)S(1)} %bitcast_multiply_fusion.1), slice={[0:2:1], [0:192:1], [1:1024:2]} | slice | bytes 1572864 | tf_op jit(solution)/shard_map/slice | solution.py:31
  501.4 31.9 %slice.890 = f32[2,192,511]{2,1,0:T(8,128)} slice(f32[2,192,1024]{2,1,0:T(8,128)S(1)} %bitcast_multiply_fusion.1), slice={[0:2:1], [0:192:1], [1:1022:2]} | slice | bytes 1569792 | tf_op jit(solution)/shard_map/slice | solution.py:31
  687.0 26.9 %pad.302 = f32[2,192,1024]{2,1,0:T(8,128)S(1)} pad(f32[2,192,512]{2,1,0:T(8,128)} %pad_maximum_fusion.10, f32[]{:T(128)} %constant.8.clone.1), padding=0_0_0x0_0_0x0_1_1 | pad | bytes 2359300 | tf_op jit(solution)/shard_map/pad | solution.py:31
  713.9 29.3 %pad.303 = f32[2,192,1024]{2,1,0:T(8,128)} pad(f32[2,192,512]{2,1,0:T(8,128)} %add.507, f32[]{:T(128)} %constant.8.clone.1), padding=0_0_0x0_0_0x1_0_1 | pad | bytes 2359300 | tf_op jit(solution)/shard_map/pad | solution.py:31
  747.3 29.2 %pad.282 = f32[2,192,1024]{2,1,0:T(8,128)} pad(f32[2,192,512]{2,1,0:T(8,128)} %pad_maximum_fusion.9, f32[]{:T(128)} %constant.8.clone.1), padding=0_0_0x0_0_0x0_1_1 | pad | bytes 2359300 | tf_op jit(solution)/shard_map/pad | solution.py:31
  776.5 29.2 %pad.283 = f32[2,192,1024]{2,1,0:T(8,128)} pad(f32[2,192,512]{2,1,0:T(8,128)} %add.477, f32[]{:T(128)} %constant.8.clone.1), padding=0_0_0x0_0_0x1_0_1 | pad | bytes 2359300 | tf_op jit(solution)/shard_map/pad | solution.py:31
  810.6 17.1 rev.18
  904.6 16.8 slice.733
  921.4 16.8 slice.735
  938.3 16.3 slice.731
  991.5 32.5 %slice.907 = f32[2,192,512]{2,1,0:T(8,128)} slice(f32[2,192,1024]{2,1,0:T(8,128)} %bitcast_multiply_fusion), slice={[0:2:1], [0:192:1], [0:1023:2]} | slice | bytes 1572864 | tf_op jit(solution)/shard_map/slice | solution.py:31
  1024.0 32.2 %slice.905 = f32[2,192,512]{2,1,0:T(8,128)} slice(f32[2,192,1024]{2,1,0:T(8,128)} %bitcast_multiply_fusion), slice={[0:2:1], [0:192:1], [1:1024:2]} | slice | bytes 1572864 | tf_op jit(solution)/shard_map/slice | solution.py:31
  1317.3 32.6 %slice.952 = f32[2,192,511]{2,1,0:T(8,128)} slice(f32[2,192,1024]{2,1,0:T(8,128)} %bitcast_multiply_fusion), slice={[0:2:1], [0:192:1], [1:1022:2]} | slice | bytes 1569792 | tf_op jit(solution)/shard_map/slice | solution.py:31
  1611.3 28.8 %pad.322 = f32[2,192,1024]{2,1,0:T(8,128)} pad(f32[2,192,512]{2,1,0:T(8,128)} %pad_maximum_fusion.11, f32[]{:T(128)} %constant.8.clone.1), padding=0_0_0x0_0_0x0_1_1 | pad | bytes 2359300 | tf_op jit(solution)/shard_map/pad | solution.py:31
  1640.1 29.4 %pad.323 = f32[2,192,1024]{2,1,0:T(8,128)} pad(f32[2,192,512]{2,1,0:T(8,128)} %add.540, f32[]{:T(128)} %constant.8.clone.1), padding=0_0_0x0_0_0x1_0_1 | pad | bytes 2359300 | tf_op jit(solution)/shard_map/pad | solution.py:31
  1674.2 29.1 %pad.262 = f32[2,192,1024]{2,1,0:T(8,128)} pad(f32[2,192,512]{2,1,0:T(8,128)} %pad_maximum_fusion.8, f32[]{:T(128)} %constant.8.clone.1), padding=0_0_0x0_0_0x0_1_1 | pad | bytes 2359300 | tf_op jit(solution)/shard_map/pad | solution.py:31
  1703.3 29.2 %pad.263 = f32[2,192,1024]{2,1,0:T(8,128)} pad(f32[2,192,512]{2,1,0:T(8,128)} %add.466, f32[]{:T(128)} %constant.8.clone.1), padding=0_0_0x0_0_0x1_0_1 | pad | bytes 2359300 | tf_op jit(solution)/shard_map/pad | solution.py:31
  1737.5 17.0 rev.19
  1754.5 17.0 rev.16
  1783.7 26.0 %all-to-all-done.7 = f32[2,192,1024]{1,0,2:T(2,128)} async-done(((f32[2,192,1024]{1,0,2:T(2,128)}), f32[2,192,1024]{1,0,2:T(2,128)}, u32[]{:S(2)}, u32[]{:S(2)}) %all-to-all-start.7) | async-done | bytes 1572896 | tf_op jit(solution)/shard_map/all_to_all | solution.py:81
  (646 shorter events, 1236.1 us)
Async XLA Ops:
  2.1 17.2 all-to-all-start.1
  19.3 16.4 all-to-all-start.2
  35.8 12.0 all-to-all-start.3
  47.8 39.0 %all-to-all-start = ((f32[2,1536,128]{2,0,1:T(2,128)}), f32[2,1536,128]{2,0,1:T(2,128)}, u32[]{:S(2)}, u32[]{:S(2)}) async-start(f32[2,1536,128]{2,0,1:T(2,128)} %bitcast), calls=%async_computation | async-start | bytes 3145728 | tf_op jit(solution)/shard_map/all_to_all | solution.py:104
  71.5 4.0 collective-permute-start.1
  74.0 5.7 collective-permute-start
  86.8 93.6 %all-to-all-start.4 = ((f32[2,1536,128]{2,0,1:T(2,128)}), f32[2,1536,128]{2,0,1:T(2,128)S(1)}, u32[]{:S(2)}, u32[]{:S(2)}) async-start(f32[2,1536,128]{2,0,1:T(2,128)} %copy.218), calls=%async_computation.4 | async-start | bytes 3145728 | tf_op jit(solution)/shard_map/all_to_all | solution.py:71
  328.1 38.1 %copy-start.36 = (f32[2,192,256]{2,1,0:T(8,128)}, f32[2,192,256]{2,1,0:T(8,128)S(1)}, u32[]{:S(2)}) copy-start(f32[2,192,256]{2,1,0:T(8,128)S(1)} %get-tuple-element.180) | copy-start | bytes 1179652
  375.6 21.5 %copy-start.12 = (f32[2,192,128]{2,1,0:T(8,128)}, f32[2,192,128]{2,1,0:T(8,128)S(1)}, u32[]{:S(2)}) copy-start(f32[2,192,128]{2,1,0:T(8,128)S(1)} %get-tuple-element.255) | copy-start | bytes 589828
  375.6 21.5 %copy-start.17 = (f32[2,192,128]{2,1,0:T(8,128)}, f32[2,192,128]{2,1,0:T(8,128)S(1)}, u32[]{:S(2)}) copy-start(f32[2,192,128]{2,1,0:T(8,128)S(1)} %get-tuple-element.254) | copy-start | bytes 589828
  646.7 22.2 %copy-start.57 = (f32[2,192,255]{2,1,0:T(8,128)S(1)}, f32[2,192,255]{2,1,0:T(8,128)}, u32[]{:S(2)}) copy-start(f32[2,192,255]{2,1,0:T(8,128)} %get-tuple-element.178) | copy-start | bytes 1175044
  843.9 31.4 %all-to-all-start.5 = ((f32[2,192,1024]{1,0,2:T(2,128)}), f32[2,192,1024]{1,0,2:T(2,128)}, u32[]{:S(2)}, u32[]{:S(2)}) async-start(f32[2,192,1024]{1,0,2:T(2,128)} %copy.233), calls=%async_computation.5 | async-start | bytes 4194304 | tf_op jit(solution)/shard_map/all_to_all | solution.py:81
  881.6 4.0 collective-permute-start.3
  884.1 5.9 collective-permute-start.2
  897.1 91.4 %all-to-all-start.6 = ((f32[2,1536,128]{2,0,1:T(2,128)}), f32[2,1536,128]{2,0,1:T(2,128)}, u32[]{:S(2)}, u32[]{:S(2)}) async-start(f32[2,1536,128]{2,0,1:T(2,128)} %copy.239), calls=%async_computation.6 | async-start | bytes 3145728 | tf_op jit(solution)/shard_map/all_to_all | solution.py:71
  1139.2 38.1 %copy-start.37 = (f32[2,192,256]{2,1,0:T(8,128)}, f32[2,192,256]{2,1,0:T(8,128)S(1)}, u32[]{:S(2)}) copy-start(f32[2,192,256]{2,1,0:T(8,128)S(1)} %get-tuple-element.176) | copy-start | bytes 1179652
  1186.8 21.5 %copy-start.14 = (f32[2,192,128]{2,1,0:T(8,128)}, f32[2,192,128]{2,1,0:T(8,128)S(1)}, u32[]{:S(2)}) copy-start(f32[2,192,128]{2,1,0:T(8,128)S(1)} %get-tuple-element.220) | copy-start | bytes 589828
  1186.8 21.5 %copy-start.19 = (f32[2,192,128]{2,1,0:T(8,128)}, f32[2,192,128]{2,1,0:T(8,128)S(1)}, u32[]{:S(2)}) copy-start(f32[2,192,128]{2,1,0:T(8,128)S(1)} %get-tuple-element.219) | copy-start | bytes 589828
  1312.5 39.2 %copy-start.71 = (f32[2,192,1]{2,1,0:T(8,128)S(1)}, f32[2,192,1]{2,1,0:T(8,128)}, u32[]{:S(2)}) copy-start(f32[2,192,1]{2,1,0:T(8,128)} %get-tuple-element.200) | copy-start | bytes 4612
  1391.0 17.5 copy-start.34
  1433.5 18.9 %copy-start.22 = (f32[2,192,64]{2,1,0:T(8,128)S(1)}, f32[2,192,64]{2,1,0:T(8,128)}, u32[]{:S(2)}) copy-start(f32[2,192,64]{2,1,0:T(8,128)} %get-tuple-element.218) | copy-start | bytes 294916
  1462.0 21.9 %copy-start.48 = (f32[2,192,128]{2,1,0:T(8,128)S(1)}, f32[2,192,128]{2,1,0:T(8,128)}, u32[]{:S(2)}) copy-start(f32[2,192,128]{2,1,0:T(8,128)} %pad.317) | copy-start | bytes 589828
  1563.7 24.8 %copy-start.58 = (f32[2,192,255]{2,1,0:T(8,128)S(1)}, f32[2,192,255]{2,1,0:T(8,128)}, u32[]{:S(2)}) copy-start(f32[2,192,255]{2,1,0:T(8,128)} %get-tuple-element.174) | copy-start | bytes 1175044
  1778.7 31.0 %all-to-all-start.7 = ((f32[2,192,1024]{1,0,2:T(2,128)}), f32[2,192,1024]{1,0,2:T(2,128)}, u32[]{:S(2)}, u32[]{:S(2)}) async-start(f32[2,192,1024]{1,0,2:T(2,128)} %copy.254), calls=%async_computation.7 | async-start | bytes 4194304 | tf_op jit(solution)/shard_map/all_to_all | solution.py:81
  (77 other events, 398.5 us)
where the time goes:
time: 1840 us; the launch traced here: 1810 us
  local copies, waits for them, and re-layouts  1530 us (83%)
  other arithmetic  174 us (9%)
  waiting for transfers between devices  50.8 us (3%)
  starting transfers between devices  48.1 us (3%)
    slice x125, local copies, waits for them, and re-layouts, suffix_maps(): lax.associative_scan(reverse_pair, (retain, source), reverse=True, axis=s...  813 us
    pad x72, local copies, waits for them, and re-layouts, suffix_maps(): lax.associative_scan(reverse_pair, (retain, source), reverse=True, axis=s...  516 us
    rev x4, local copies, waits for them, and re-layouts, suffix_maps(): lax.associative_scan(reverse_pair, (retain, source), reverse=True, axis=s...  62.8 us
    unnamed x203, local copies, waits for them, and re-layouts  55.9 us
    add x39, other arithmetic, suffix_maps(): lax.associative_scan(reverse_pair, (retain, source), reverse=True, axis=s...  51.6 us
    add x38, other arithmetic, compose(): outer_map[0] * inner_map[1] + outer_map[1]  50.6 us
  transfers between devices with their start and end apart: 12, of which 8 were waited for; matrix products, arithmetic and copies ran while one was open for 13% of the time, Pallas kernels for 0%

commit v1 on v0

v1 whole, which is shorter than its diff:
```python
import functools

import jax
import jax.numpy as jnp
from jax import lax
from jax.experimental import pallas as pl
from jax.experimental.pallas import tpu as pltpu
from jax.sharding import PartitionSpec as P

MESH = pl.DeviceIdType.MESH
SUB = 8
LANES = 128
PAD = 8
F32 = jnp.float32
BF16 = jnp.bfloat16


def kernel(
    dims,
    east_hbm, north_hbm, kern_ref, dep_ref, cells_ref, counts_ref,
    out_ref, flux_ref,
    weight, faces, gain_t, gain_levels, field, rows, rows_t, forcing,
    features, sent, stage_lon, stage_lat, got_t, term_hi, term_lo, left, onehot,
    edge_out, edge_in, face_out, face_in, gain_all, rest_all,
    local_sem, lon_send, lon_recv, lat_send, lat_recv, gain_send, gain_recv,
    rest_send, rest_recv, edge_send, edge_recv, face_sem,
):
    steps, tracers, levels, lat_rows, n_lat, n_lon, slots, capacity = dims
    merged = levels * lat_rows
    blocks = merged // LANES
    seg = LANES // SUB
    half = lat_rows // 2
    fields = tracers * levels
    my_lat, my_lon = lax.axis_index("lat"), lax.axis_index("lon")
    has_up = my_lat < n_lat - 1
    has_down = my_lat > 0

    def lon_peer(k):
        return (my_lat, lax.rem(my_lon + k, n_lon))

    def lat_peer(k):
        return (lax.rem(my_lat + k, n_lat), my_lon)

    def remote(src, dst, send, recv, device):
        return pltpu.make_async_remote_copy(
            src_ref=src, dst_ref=dst, send_sem=send, recv_sem=recv,
            device_id=device, device_id_type=MESH,
        )

    load_east = pltpu.make_async_copy(east_hbm, weight, local_sem.at[0])
    load_east.start()
    load_north = pltpu.make_async_copy(
        north_hbm, faces.at[:, :, pl.ds(PAD, lat_rows), :], local_sem.at[1]
    )
    load_north.start()

    gain_all[...] = jnp.zeros_like(gain_all)
    rest_all[...] = jnp.zeros_like(rest_all)
    face_in[...] = jnp.zeros_like(face_in)
    edge_in[...] = jnp.zeros_like(edge_in)
    barrier = pltpu.get_barrier_semaphore()
    for k in range(1, n_lon):
        pl.semaphore_signal(barrier, inc=1, device_id=lon_peer(k), device_id_type=MESH)
    for k in range(1, n_lat):
        pl.semaphore_signal(barrier, inc=1, device_id=lat_peer(k), device_id_type=MESH)

    owners = n_lat * n_lon
    spread = (
        lax.broadcasted_iota(jnp.int32, (owners, slots), 1) // capacity
        == lax.broadcasted_iota(jnp.int32, (owners, slots), 0)
    ).astype(F32)
    counts = jnp.dot(counts_ref[...].astype(F32), spread, preferred_element_type=F32)
    within = lax.rem(lax.broadcasted_iota(jnp.int32, (steps, slots), 1), capacity).astype(F32)
    live = (within < counts).astype(F32)
    features[...] = jnp.zeros_like(features)
    dep_row = steps * levels
    cell_row = dep_row + steps * tracers
    for n in range(steps):
        features[n * levels:(n + 1) * levels, :] = kern_ref[n]
        for t in range(tracers):
            at = dep_row + n * tracers + t
            features[at:at + 1, :] = dep_ref[n, t:t + 1, :] * live[n:n + 1, :]
        features[cell_row + n:cell_row + n + 1, :] = cells_ref[n:n + 1, :].astype(F32)
    by_slot = features[...].T
    for p in range(n_lat):
        for q in range(n_lon):
            at = (p * n_lon + q) * capacity
            sent[q, p] = by_slot[at:at + capacity]
    pl.semaphore_wait(barrier, n_lon - 1 + n_lat - 1)

    lon_copies = [
        remote(sent.at[lax.rem(my_lon + k, n_lon)], stage_lon.at[k],
               lon_send.at[k], lon_recv.at[k], lon_peer(k))
        for k in range(1, n_lon)
    ]
    for copy in lon_copies:
        copy.start()
    stage_lon[0] = sent[my_lon]

    load_north.wait()
    face_out[...] = faces[:, :, PAD + lat_rows - 1, :]
    up_device = (lax.rem(my_lat + 1, n_lat), my_lon)
    down_device = (lax.rem(my_lat + n_lat - 1, n_lat), my_lon)
    face_copy = remote(face_out, face_in, face_sem.at[0], face_sem.at[1], up_device)

    @pl.when(has_up)
    def _():
        face_copy.start()

    @pl.when(jnp.logical_not(has_up))
    def _():
        faces[:, :, PAD + lat_rows - 1, :] = jnp.zeros((steps, levels, LANES), F32)

    sub = lax.rem(lax.broadcasted_iota(jnp.int32, (blocks * SUB, LANES), 0), SUB)

    def ahead(x, d):
        return pltpu.roll(x, blocks * SUB - d, 0)

    def flat(x):
        return x.reshape(blocks * SUB, LANES)

    def gains(n):
        def one(b, carry):
            at = pl.ds(pl.multiple_of(b * LANES, LANES), LANES)
            east = weight[n, at, :]
            share = 1.0 / (1.0 + east)
            weight[n, at, :] = share
            gain_t[n, b] = (east * share).T
            return carry

        lax.fori_loop(0, blocks, one, 0, unroll=2)
        g = gain_t[n, :, pl.ds(seg - 1, SUB, stride=seg), :]
        for p in range(seg - 2, -1, -1):
            g = g * gain_t[n, :, pl.ds(p, SUB, stride=seg), :]
        g = flat(g)
        for level, d in enumerate((1, 2, 4)):
            gain_levels[n, level] = g
            g = jnp.where(sub < SUB - d, g * ahead(g, d), g)
        gain_levels[n, 3] = g
        for b in range(blocks):
            gain_all[0, n, b:b + 1, :] = g[b * SUB:b * SUB + 1, :]

    load_east.wait()
    gains(steps - 1)

    for copy in lon_copies:
        copy.wait()
    lat_copies = [
        remote(stage_lon.at[:, lax.rem(my_lat + k, n_lat)], stage_lat.at[k],
               lat_send.at[k], lat_recv.at[k], lat_peer(k))
        for k in range(1, n_lat)
    ]
    for copy in lat_copies:
        copy.start()
    stage_lat[0] = stage_lon[:, my_lat]
    for n in range(steps - 2, -1, -1):
        gains(n)
    gain_copies = [
        remote(gain_all.at[0], gain_all.at[k], gain_send.at[k], gain_recv.at[k], lon_peer(k))
        for k in range(1, n_lon)
    ]
    for copy in gain_copies:
        copy.start()
    for copy in lat_copies:
        copy.wait()

    got = stage_lat[...].reshape(slots, LANES)
    got_t[...] = got.T
    group = SUB
    shift = LANES.bit_length() - 1

    def split_cell(cell):
        row = lax.shift_right_logical(cell, shift)
        upper = (row >= half).astype(jnp.int32)
        return row - half * upper, (cell & (LANES - 1)) + LANES * upper

    def deposit(n, store):
        for t in range(tracers):
            at = dep_row + n * tracers + t
            term = got_t[at:at + 1, :] * got_t[n * levels:(n + 1) * levels, :]
            high = term.astype(BF16).astype(F32)
            term_hi[t * levels:(t + 1) * levels, :] = high
            term_lo[t * levels:(t + 1) * levels, :] = term - high
        lane_cell = got_t[cell_row + n:cell_row + n + 1, :].astype(jnp.int32)
        slot_row, _ = split_cell(lane_cell)
        _, slot_col = split_cell(stage_lat[...].reshape(slots, LANES)[
            :, cell_row + n:cell_row + n + 1].astype(jnp.int32))
        hot = (
            lax.broadcasted_iota(jnp.int32, (slots, 2 * LANES), 1) == slot_col
        ).astype(F32).astype(BF16)
        onehot[0:slots, :] = hot
        onehot[slots:2 * slots, :] = hot
        here = lax.broadcasted_iota(jnp.int32, (half, slots), 0) == slot_row

        def one(c, carry):
            for i in range(group):
                at = pl.ds(c * group + i, 1)
                part = pl.ds(i * half, half)
                left[part, 0:slots] = jnp.where(here, term_hi[at, :], 0.0).astype(BF16)
                left[part, slots:2 * slots] = jnp.where(here, term_lo[at, :], 0.0).astype(BF16)
            added = jnp.dot(left[...], onehot[...], preferred_element_type=F32)
            for i in range(group):
                block = added[i * half:(i + 1) * half]
                store(c * group + i, block[:, :LANES], block[:, LANES:])
            return carry

        lax.fori_loop(0, fields // group, one, 0)

    def into_field(i, low, high):
        field[i, PAD:PAD + half, :] = low
        field[i, PAD + half:PAD + lat_rows, :] = high

    def into_forcing(n):
        def store(i, low, high):
            forcing[n, i, 0:half, :] = low
            forcing[n, i, half:lat_rows, :] = high
        return store

    deposit(steps - 1, into_field)

    for n in range(steps - 1, -1, -1):
        edge_out[n, 0] = field[:, PAD, :]
        edge_out[n, 1] = field[:, PAD + lat_rows - 1, :]
        to_up = remote(edge_out.at[n, 1], edge_in.at[n, 0], edge_send.at[n, 1], edge_recv.at[n, 0], up_device)
        to_down = remote(edge_out.at[n, 0], edge_in.at[n, 1], edge_send.at[n, 0], edge_recv.at[n, 1], down_device)

        @pl.when(has_up)
        def _():
            to_up.start()

        @pl.when(has_down)
        def _():
            to_down.start()

        for t in range(tracers):
            surface = field[t * levels, PAD:PAD + lat_rows, :]
            if n == steps - 1:
                flux_ref[t] = surface
            else:
                flux_ref[t] = flux_ref[t] + surface
        if n == steps - 1:
            for m in range(steps - 2, -1, -1):
                deposit(m, into_forcing(m))

            @pl.when(has_down)
            def _():
                face_copy.wait_recv()

            @pl.when(has_up)
            def _():
                face_copy.wait_send()

            faces[:, :, PAD - 1, :] = face_in[...]

        @pl.when(has_up)
        def _():
            to_up.wait_send()
            to_down.wait_recv()

        @pl.when(has_down)
        def _():
            to_down.wait_send()
            to_up.wait_recv()

        field[:, PAD - 1, :] = edge_in[n, 0]
        field[:, PAD + lat_rows, :] = edge_in[n, 1]

        def lat_step(l, carry):
            northward = jnp.maximum(faces[n, l, PAD:PAD + lat_rows, :], 0.0)
            southward = jnp.minimum(faces[n, l, PAD - 1:PAD - 1 + lat_rows, :], 0.0)
            share = weight[n, pl.ds(pl.multiple_of(l * lat_rows, SUB), lat_rows), :]
            for t in range(tracers):
                i = t * levels + l
                a = field[i, PAD:PAD + lat_rows, :]
                above = field[i, PAD + 1:PAD + 1 + lat_rows, :]
                below = field[i, PAD - 1:PAD - 1 + lat_rows, :]
                y = a + northward * (above - a) + southward * (a - below)
                rows[pl.ds(pl.multiple_of(i * lat_rows, SUB), lat_rows), :] = share * y
            return carry

        lax.fori_loop(0, levels, lat_step, 0)

        def turn(b, carry):
            rows_t[b] = rows[pl.ds(pl.multiple_of(b * LANES, LANES), LANES), :].T
            return carry

        lax.fori_loop(0, tracers * blocks, turn, 0, unroll=4)

        def gain_at(p):
            return gain_t[n, :, pl.ds(p, SUB, stride=seg), :]

        def row_at(t, p):
            return (pl.ds(t * blocks, blocks), pl.ds(p, SUB, stride=seg), slice(None))

        rest = [rows_t[row_at(t, seg - 1)] for t in range(tracers)]
        for p in range(seg - 2, -1, -1):
            r = gain_at(p)
            rest = [r * s + rows_t[row_at(t, p)] for t, s in enumerate(rest)]
        rest = [flat(s) for s in rest]
        for level, d in enumerate((1, 2, 4)):
            g = gain_levels[n, level]
            rest = [jnp.where(sub < SUB - d, s + g * ahead(s, d), s) for s in rest]
        for t in range(tracers):
            for b in range(blocks):
                rest_all[n, 0, t, b:b + 1, :] = rest[t][b * SUB:b * SUB + 1, :]
        rest_copies = [
            remote(rest_all.at[n, 0], rest_all.at[n, k], rest_send.at[n, k], rest_recv.at[n, k], lon_peer(k))
            for k in range(1, n_lon)
        ]
        for copy in rest_copies:
            copy.start()
        if n == steps - 1:
            for copy in gain_copies:
                copy.wait()
        whole = gain_all[0, n]
        for k in range(1, n_lon):
            whole = whole * gain_all[k, n]
        for copy in rest_copies:
            copy.wait()
        ends = []
        for t in range(tracers):
            total = rest_all[n, 0, t]
            for k in range(1, n_lon):
                total = rest_all[n, k, t] + gain_all[k, n] * total
            closure = total / (1.0 - whole)
            wide = jnp.concatenate(
                [jnp.broadcast_to(closure[b:b + 1, :], (SUB, LANES)) for b in range(blocks)], 0
            )
            inclusive = gain_levels[n, 3] * wide + rest[t]
            end = jnp.where(sub == SUB - 1, wide, ahead(inclusive, 1))
            ends.append(end.reshape(blocks, SUB, LANES))
        for p in range(seg - 1, -1, -1):
            r = gain_at(p)
            for t in range(tracers):
                ends[t] = r * ends[t] + rows_t[row_at(t, p)]
                rows_t[row_at(t, p)] = ends[t]

        target = rows if n > 0 else out_ref

        def turn_back(b, carry):
            target[pl.ds(pl.multiple_of(b * LANES, LANES), LANES), :] = rows_t[b].T
            return carry

        lax.fori_loop(0, tracers * blocks, turn_back, 0, unroll=4)

        if n > 0:
            def add(i, carry):
                solved = rows[pl.ds(pl.multiple_of(i * lat_rows, SUB), lat_rows), :]
                field[i, PAD:PAD + lat_rows, :] = solved + forcing[n - 1, i]
                return carry

            lax.fori_loop(0, fields, add, 0, unroll=2)


def shards(east_courant, north_courant, kernels, departures, cells, counts):
    steps, levels, lat_rows, lon_cells = east_courant.shape
    tracers = departures.shape[1]
    n_lat, n_lon = lax.axis_size("lat"), lax.axis_size("lon")
    owners = n_lat * n_lon
    slots = cells.shape[1]
    capacity = slots // owners
    merged = levels * lat_rows
    blocks = merged // LANES
    padded = -(-blocks // SUB) * SUB
    fields = tracers * levels
    dims = (steps, tracers, levels, lat_rows, n_lat, n_lon, slots, capacity)
    vmem = pltpu.VMEM
    dma = pltpu.SemaphoreType.DMA
    whole = pl.BlockSpec(memory_space=pltpu.VMEM)
    anywhere = pl.BlockSpec(memory_space=pl.ANY)
    state, flux = pl.pallas_call(
        functools.partial(kernel, dims),
        out_shape=(
            jax.ShapeDtypeStruct((tracers * merged, lon_cells), F32),
            jax.ShapeDtypeStruct((tracers, lat_rows, lon_cells), F32),
        ),
        in_specs=[anywhere, anywhere, whole, whole, whole, whole],
        out_specs=(whole, whole),
        scratch_shapes=[
            vmem((steps, merged, LANES), F32),
            vmem((steps, levels, lat_rows + PAD, LANES), F32),
            vmem((steps, blocks, LANES, LANES), F32),
            vmem((steps, 4, blocks * SUB, LANES), F32),
            vmem((fields, lat_rows + 2 * PAD, LANES), F32),
            vmem((tracers * merged, LANES), F32),
            vmem((tracers * blocks, LANES, LANES), F32),
            vmem((max(steps - 1, 1), fields, lat_rows, LANES), F32),
            vmem((LANES, slots), F32),
            vmem((n_lon, n_lat, capacity, LANES), F32),
            vmem((n_lon, n_lat, capacity, LANES), F32),
            vmem((n_lat, n_lon, capacity, LANES), F32),
            vmem((LANES, slots), F32),
            vmem((fields, slots), F32),
            vmem((fields, slots), F32),
            vmem((SUB * lat_rows // 2, 2 * slots), BF16),
            vmem((2 * slots, 2 * LANES), BF16),
            vmem((steps, 2, fields, LANES), F32),
            vmem((steps, 2, fields, LANES), F32),
            vmem((steps, levels, LANES), F32),
            vmem((steps, levels, LANES), F32),
            vmem((n_lon, steps, padded, LANES), F32),
            vmem((steps, n_lon, tracers, padded, LANES), F32),
            dma((2,)),
            dma((n_lon,)), dma((n_lon,)),
            dma((n_lat,)), dma((n_lat,)),
            dma((n_lon,)), dma((n_lon,)),
            dma((steps, n_lon)), dma((steps, n_lon)),
            dma((steps, 2)), dma((steps, 2)),
            dma((2,)),
        ],
        compiler_params=pltpu.CompilerParams(
            collective_id=0, has_side_effects=True, vmem_limit_bytes=48 * 1024 * 1024
        ),
        name="adjoint_window",
    )(
        east_courant.reshape(steps, merged, lon_cells), north_courant,
        kernels, departures, cells, counts,
    )
    return state.reshape(tracers, levels, lat_rows, lon_cells), flux


def solution(mesh):
    return jax.shard_map(
        shards,
        mesh=mesh,
        in_specs=(
            P(None, None, "lat", "lon"),
            P(None, None, "lat", "lon"),
            P(None, None, ("lat", "lon")),
            P(None, None, ("lat", "lon")),
            P(None, ("lat", "lon")),
            P(None, ("lat", "lon")),
        ),
        out_specs=(P(None, None, "lat", "lon"), P(None, "lat", "lon")),
        check_vma=False,
    )
```

time: 1840 us -> 44.8 us (0.02); the launches traced: 1810 us -> 44.5 us
  local copies, waits for them, and re-layouts: 1530 us -> 7.4 us
  other arithmetic: 174 us -> 0 us
  waiting for transfers between devices: 50.8 us -> 0 us
  starting transfers between devices: 48.1 us -> 0 us
  Pallas kernels: 0 us -> 36.4 us
    slice x131 -> x0, local copies, waits for them, and re-layouts: 826 us -> none  [the longest x125 813 us: suffix_maps(): lax.associative_scan(reverse_pair, (retain, source), reverse=True, axis=s...]
    pad x72 -> x0, local copies, waits for them, and re-layouts: 516 us -> none  [suffix_maps(): lax.associative_scan(reverse_pair, (retain, source), reverse=True, axis=s...]
    add x95 -> x0, other arithmetic: 119 us -> none  [the longest x39 51.6 us: suffix_maps(): lax.associative_scan(reverse_pair, (retain, source), reverse=True, axis=s...]
    rev x4 -> x0, local copies, waits for them, and re-layouts: 62.8 us -> none  [suffix_maps(): lax.associative_scan(reverse_pair, (retain, source), reverse=True, axis=s...]
    unnamed x203 -> x14, local copies, waits for them, and re-layouts: 55.9 us -> 7.4 us
    all_to_all x8 -> x0, waiting for transfers between devices: 42.1 us -> none  [the longest x2 34.1 us: pencil_solve(): lax.all_to_all(solved, 'lon', split_axis=2, concat_axis=1, tiled=True)]
    all_to_all x8 -> x0, starting transfers between devices: 40.4 us -> none  [the longest x2 9.11 us: pencil_solve(): lax.all_to_all(solved, 'lon', split_axis=2, concat_axis=1, tiled=True)]
    pallas_call x0 -> x1, Pallas kernels: none -> 36.4 us  [shards(): pl.pallas_call(functools.partial(kernel, dims), out_shape=(jax.ShapeDtype...]
  transfers between devices with their start and end apart: 12 -> 0, of which waited for: 8 -> 0; matrix products, arithmetic and copies ran while one was open for 13% -> 0% of each run, Pallas kernels for 0% -> 0%
where the time goes in v1:
time: 44.8 us; the launch traced here: 44.5 us
  Pallas kernels  36.4 us (81%)
  local copies, waits for them, and re-layouts  7.4 us (17%)
  between operations  0.65 us (1%)
    pallas_call x1, Pallas kernels, shards(): pl.pallas_call(functools.partial(kernel, dims), out_shape=(jax.ShapeDtype...  36.4 us
    unnamed x14, local copies, waits for them, and re-layouts  7.4 us

profile of v1, /device:TPU:0, one launch (start us, length us, event | category | flops | bytes accessed | tf_op | source)
XLA Modules:
  0.0 44.5 jit_solution(8902122492355857911)
XLA Ops:
  0.6 0.0 copy-start
  0.6 1.4 %copy-done = f32[2,16,96,128]{3,2,1,0:T(8,128)S(1)} copy-done((f32[2,16,96,128]{3,2,1,0:T(8,128)S(1)}, f32[2,16,96,128]{3,2,1,0:T(8,128)}, u32[]{:S(2)}) %copy-start) | copy-done | bytes 1572888
  2.0 0.0 copy-start.1
  2.0 1.4 %copy-done.1 = f32[2,16,96,128]{3,2,1,0:T(8,128)S(1)} copy-done((f32[2,16,96,128]{3,2,1,0:T(8,128)S(1)}, f32[2,16,96,128]{3,2,1,0:T(8,128)}, u32[]{:S(2)}) %copy-start.1) | copy-done | bytes 1572888
  3.4 0.0 copy-start.2
  3.5 0.8 %copy-done.2 = f32[2,16,256]{2,1,0:T(8,128)S(1)} copy-done((f32[2,16,256]{2,1,0:T(8,128)S(1)}, f32[2,16,256]{2,1,0:T(8,128)}, u32[]{:S(2)}) %copy-start.2) | copy-done | bytes 32792
  4.2 0.0 copy-start.3
  4.2 0.7 %copy-done.3 = f32[2,2,256]{2,1,0:T(2,128)S(1)} copy-done((f32[2,2,256]{2,1,0:T(2,128)S(1)}, f32[2,2,256]{2,1,0:T(2,128)}, u32[]{:S(2)}) %copy-start.3) | copy-done | bytes 4120
  4.9 0.0 copy-start.4
  4.9 0.7 %copy-done.4 = s32[2,256]{1,0:T(2,128)S(1)} copy-done((s32[2,256]{1,0:T(2,128)S(1)}, s32[2,256]{1,0:T(2,128)}, u32[]{:S(2)}) %copy-start.4) | copy-done | bytes 2072
  5.6 0.0 copy-start.5
  5.6 0.7 %copy-done.5 = s32[2,32]{1,0:T(2,128)S(1)} copy-done((s32[2,32]{1,0:T(2,128)S(1)}, s32[2,32]{1,0:T(2,128)}, u32[]{:S(2)}) %copy-start.5) | copy-done | bytes 280
  6.3 36.4 %adjoint_window.1 = (f32[3072,128]{1,0:T(8,128)S(1)}, f32[2,96,128]{2,1,0:T(8,128)S(1)}) custom-call(f32[2,1536,128]{2,1,0:T(8,128)S(1)} %bitcast.2, f32[2,16,96,128]{3,2,1,0:T(8,128)S(1)} %copy-done.1, f32[2,16,256]{2,1,0:T(8,128)S(1)} %copy-done.2, f32[2,2,256]{2,1,0:T(2,128)S(1)} %copy-done.3, s32[2,256]{1,0:T(2,128)S(1)} %copy-done.4, s32[2,32]{1,0:T(2,128)S(1)} %copy-done.5), custom_call_target="tpu_custom_call" | custom-call | tf_op jit(solution)/shard_map/adjoint_window/pallas_call | solution.py:371
  42.7 1.1 %copy.10 = f32[2,16,96,128]{3,2,1,0:T(8,128)} copy(f32[2,16,96,128]{3,2,1,0:T(8,128)S(1)} %bitcast.3) | data formatting | bytes 3145728
  43.8 0.6 %copy.11 = f32[2,96,128]{2,1,0:T(8,128)} copy(f32[2,96,128]{2,1,0:T(8,128)S(1)} %get-tuple-element.9) | data formatting | bytes 196608
Async XLA Ops:
  0.6 1.4 %copy-start = (f32[2,16,96,128]{3,2,1,0:T(8,128)S(1)}, f32[2,16,96,128]{3,2,1,0:T(8,128)}, u32[]{:S(2)}) copy-start(f32[2,16,96,128]{3,2,1,0:T(8,128)} %param.6) | copy-start | bytes 4718596
  2.0 1.4 %copy-start.1 = (f32[2,16,96,128]{3,2,1,0:T(8,128)S(1)}, f32[2,16,96,128]{3,2,1,0:T(8,128)}, u32[]{:S(2)}) copy-start(f32[2,16,96,128]{3,2,1,0:T(8,128)} %north_hbm.1) | copy-start | bytes 4718596
  3.4 0.8 %copy-start.2 = (f32[2,16,256]{2,1,0:T(8,128)S(1)}, f32[2,16,256]{2,1,0:T(8,128)}, u32[]{:S(2)}) copy-start(f32[2,16,256]{2,1,0:T(8,128)} %kern_ref.1) | copy-start | bytes 98308
  4.2 0.7 %copy-start.3 = (f32[2,2,256]{2,1,0:T(2,128)S(1)}, f32[2,2,256]{2,1,0:T(2,128)}, u32[]{:S(2)}) copy-start(f32[2,2,256]{2,1,0:T(2,128)} %dep_ref.1) | copy-start | bytes 12292
  4.9 0.7 %copy-start.4 = (s32[2,256]{1,0:T(2,128)S(1)}, s32[2,256]{1,0:T(2,128)}, u32[]{:S(2)}) copy-start(s32[2,256]{1,0:T(2,128)} %cells_ref.1) | copy-start | bytes 6148
  5.6 0.7 %copy-start.5 = (s32[2,32]{1,0:T(2,128)S(1)}, s32[2,32]{1,0:T(2,128)}, u32[]{:S(2)}) copy-start(s32[2,32]{1,0:T(2,128)} %counts_ref.1) | copy-start | bytes 772

commit v2 on v1

--- a/solution.py
+++ b/solution.py
@@ -17,8 +17,10 @@
 
 def kernel(
     dims,
-    east_hbm, north_hbm, kern_ref, dep_ref, cells_ref, counts_ref,
-    out_ref, flux_ref,
+    east_hbm, north_hbm, kern_hbm, dep_hbm, cells_hbm, counts_hbm,
+    out_hbm, flux_hbm,
+    flux_ref,
+    kern_ref, dep_ref, cells_ref, counts_ref, edge_gain,
     weight, faces, gain_t, gain_levels, field, rows, rows_t, forcing,
     features, sent, stage_lon, stage_lat, got_t, term_hi, term_lo, left, onehot,
     edge_out, edge_in, face_out, face_in, gain_all, rest_all,
@@ -47,6 +49,14 @@
             device_id=device, device_id_type=MESH,
         )
 
+    small = [
+        pltpu.make_async_copy(src, dst, local_sem.at[2 + i])
+        for i, (src, dst) in enumerate((
+            (kern_hbm, kern_ref), (dep_hbm, dep_ref), (cells_hbm, cells_ref), (counts_hbm, counts_ref),
+        ))
+    ]
+    for copy in small:
+        copy.start()
     load_east = pltpu.make_async_copy(east_hbm, weight, local_sem.at[0])
     load_east.start()
     load_north = pltpu.make_async_copy(
@@ -58,12 +68,16 @@
     rest_all[...] = jnp.zeros_like(rest_all)
     face_in[...] = jnp.zeros_like(face_in)
     edge_in[...] = jnp.zeros_like(edge_in)
+    field[:, PAD - 1, :] = jnp.zeros((fields, LANES), F32)
+    field[:, PAD + lat_rows, :] = jnp.zeros((fields, LANES), F32)
     barrier = pltpu.get_barrier_semaphore()
     for k in range(1, n_lon):
         pl.semaphore_signal(barrier, inc=1, device_id=lon_peer(k), device_id_type=MESH)
     for k in range(1, n_lat):
         pl.semaphore_signal(barrier, inc=1, device_id=lat_peer(k), device_id_type=MESH)
 
+    for copy in small:
+        copy.wait()
     owners = n_lat * n_lon
     spread = (
         lax.broadcasted_iota(jnp.int32, (owners, slots), 1) // capacity
@@ -218,11 +232,15 @@
 
     deposit(steps - 1, into_field)
 
-    for n in range(steps - 1, -1, -1):
-        edge_out[n, 0] = field[:, PAD, :]
-        edge_out[n, 1] = field[:, PAD + lat_rows - 1, :]
-        to_up = remote(edge_out.at[n, 1], edge_in.at[n, 0], edge_send.at[n, 1], edge_recv.at[n, 0], up_device)
-        to_down = remote(edge_out.at[n, 0], edge_in.at[n, 1], edge_send.at[n, 0], edge_recv.at[n, 1], down_device)
+    def edge_copies(n, t):
+        to_up = remote(edge_out.at[n, 1, t], edge_in.at[n, 0, t],
+                       edge_send.at[n, 1, t], edge_recv.at[n, 0, t], up_device)
+        to_down = remote(edge_out.at[n, 0, t], edge_in.at[n, 1, t],
+                         edge_send.at[n, 0, t], edge_recv.at[n, 1, t], down_device)
+        return to_up, to_down
+
+    def send_edges(n, t):
+        to_up, to_down = edge_copies(n, t)
 
         @pl.when(has_up)
         def _():
@@ -232,25 +250,8 @@
         def _():
             to_down.start()
 
-        for t in range(tracers):
-            surface = field[t * levels, PAD:PAD + lat_rows, :]
-            if n == steps - 1:
-                flux_ref[t] = surface
-            else:
-                flux_ref[t] = flux_ref[t] + surface
-        if n == steps - 1:
-            for m in range(steps - 2, -1, -1):
-                deposit(m, into_forcing(m))
-
-            @pl.when(has_down)
-            def _():
-                face_copy.wait_recv()
-
-            @pl.when(has_up)
-            def _():
-                face_copy.wait_send()
-
-            faces[:, :, PAD - 1, :] = face_in[...]
+    def wait_edges(n, t):
+        to_up, to_down = edge_copies(n, t)
 
         @pl.when(has_up)
         def _():
@@ -262,94 +263,158 @@
             to_down.wait_send()
             to_up.wait_recv()
 
-        field[:, PAD - 1, :] = edge_in[n, 0]
-        field[:, PAD + lat_rows, :] = edge_in[n, 1]
-
-        def lat_step(l, carry):
+    def rest_copies(n, t):
+        return [
+            remote(rest_all.at[n, t, 0], rest_all.at[n, t, k],
+                   rest_send.at[n, t, k], rest_recv.at[n, t, k], lon_peer(k))
+            for k in range(1, n_lon)
+        ]
+
+    def bottom_rows(t, row):
+        return (pl.ds(t * merged + row, levels, stride=lat_rows), slice(None))
+
+    def add_flux(n, t):
+        surface = field[t * levels, PAD:PAD + lat_rows, :]
+        flux_ref[t] = surface if n == steps - 1 else flux_ref[t] + surface
+
+    def lat_stencil(n, t):
+        def one(l, carry):
             northward = jnp.maximum(faces[n, l, PAD:PAD + lat_rows, :], 0.0)
             southward = jnp.minimum(faces[n, l, PAD - 1:PAD - 1 + lat_rows, :], 0.0)
             share = weight[n, pl.ds(pl.multiple_of(l * lat_rows, SUB), lat_rows), :]
-            for t in range(tracers):
-                i = t * levels + l
-                a = field[i, PAD:PAD + lat_rows, :]
-                above = field[i, PAD + 1:PAD + 1 + lat_rows, :]
-                below = field[i, PAD - 1:PAD - 1 + lat_rows, :]
-                y = a + northward * (above - a) + southward * (a - below)
-                rows[pl.ds(pl.multiple_of(i * lat_rows, SUB), lat_rows), :] = share * y
+            i = t * levels + l
+            a = field[i, PAD:PAD + lat_rows, :]
+            above = field[i, PAD + 1:PAD + 1 + lat_rows, :]
+            below = field[i, PAD - 1:PAD - 1 + lat_rows, :]
+            y = a + northward * (above - a) + southward * (a - below)
+            rows[pl.ds(pl.multiple_of(i * lat_rows, SUB), lat_rows), :] = share * y
             return carry
 
-        lax.fori_loop(0, levels, lat_step, 0)
+        lax.fori_loop(0, levels, one, 0, unroll=2)
+
+    def gain_at(n, p):
+        return gain_t[n, :, pl.ds(p, SUB, stride=seg), :]
+
+    def row_at(t, p):
+        return (pl.ds(t * blocks, blocks), pl.ds(p, SUB, stride=seg), slice(None))
+
+    def block_rest(n, t):
+        for side, row in ((0, 0), (1, lat_rows - 1)):
+            at = bottom_rows(t, row)
+            rows[at] = rows[at] + edge_gain[n, side] * edge_in[n, side, t]
 
         def turn(b, carry):
+            b = b + t * blocks
             rows_t[b] = rows[pl.ds(pl.multiple_of(b * LANES, LANES), LANES), :].T
             return carry
 
-        lax.fori_loop(0, tracers * blocks, turn, 0, unroll=4)
-
-        def gain_at(p):
-            return gain_t[n, :, pl.ds(p, SUB, stride=seg), :]
-
-        def row_at(t, p):
-            return (pl.ds(t * blocks, blocks), pl.ds(p, SUB, stride=seg), slice(None))
-
-        rest = [rows_t[row_at(t, seg - 1)] for t in range(tracers)]
+        lax.fori_loop(0, blocks, turn, 0, unroll=4)
+        rest = rows_t[row_at(t, seg - 1)]
         for p in range(seg - 2, -1, -1):
-            r = gain_at(p)
-            rest = [r * s + rows_t[row_at(t, p)] for t, s in enumerate(rest)]
-        rest = [flat(s) for s in rest]
+            rest = gain_at(n, p) * rest + rows_t[row_at(t, p)]
+        rest = flat(rest)
         for level, d in enumerate((1, 2, 4)):
-            g = gain_levels[n, level]
-            rest = [jnp.where(sub < SUB - d, s + g * ahead(s, d), s) for s in rest]
+            rest = jnp.where(sub < SUB - d, rest + gain_levels[n, level] * ahead(rest, d), rest)
+        for b in range(blocks):
+            rest_all[n, t, 0, b:b + 1, :] = rest[b * SUB:b * SUB + 1, :]
+        for copy in rest_copies(n, t):
+            copy.start()
+        return rest
+
+    def finish(n, t, rest, scale):
+        for copy in rest_copies(n, t):
+            copy.wait()
+        total = rest_all[n, t, 0]
+        for k in range(1, n_lon):
+            total = rest_all[n, t, k] + gain_all[k, n] * total
+        closure = total * scale
+        wide = jnp.concatenate(
+            [jnp.broadcast_to(closure[b:b + 1, :], (SUB, LANES)) for b in range(blocks)], 0
+        )
+        inclusive = gain_levels[n, 3] * wide + rest
+        end = jnp.where(sub == SUB - 1, wide, ahead(inclusive, 1)).reshape(blocks, SUB, LANES)
+        for p in range(seg - 1, -1, -1):
+            end = gain_at(n, p) * end + rows_t[row_at(t, p)]
+            rows_t[row_at(t, p)] = end
+
+        def turn_back(b, carry):
+            b = b + t * blocks
+            rows[pl.ds(pl.multiple_of(b * LANES, LANES), LANES), :] = rows_t[b].T
+            return carry
+
+        lax.fori_loop(0, blocks, turn_back, 0, unroll=4)
+
+    def next_field(n, t):
+        some = slice(t * levels, (t + 1) * levels)
+        for side, row in ((0, 0), (1, lat_rows - 1)):
+            edge_out[n, side, t] = rows[bottom_rows(t, row)] + forcing[n, some, row, :]
+        send_edges(n, t)
+
+        def add(l, carry):
+            i = t * levels + l
+            solved = rows[pl.ds(pl.multiple_of(i * lat_rows, SUB), lat_rows), :]
+            field[i, PAD:PAD + lat_rows, :] = solved + forcing[n, i]
+            return carry
+
+        lax.fori_loop(0, levels, add, 0, unroll=2)
+        add_flux(n, t)
+        lat_stencil(n, t)
+
+    def result_copy(t):
+        some = pl.ds(t * merged, merged)
+        return pltpu.make_async_copy(rows.at[some], out_hbm.at[some], local_sem.at[6 + t])
+
+    flux_copy = pltpu.make_async_copy(flux_ref, flux_hbm, local_sem.at[6 + tracers])
+    last = steps - 1
+    for t in range(tracers):
+        some = slice(t * levels, (t + 1) * levels)
+        edge_out[last, 0, t] = field[some, PAD, :]
+        edge_out[last, 1, t] = field[some, PAD + lat_rows - 1, :]
+        send_edges(last, t)
+    for m in range(steps - 2, -1, -1):
+        deposit(m, into_forcing(m))
+
+    @pl.when(has_down)
+    def _():
+        face_copy.wait_recv()
+
+    @pl.when(has_up)
+    def _():
+        face_copy.wait_send()
+
+    faces[:, :, PAD - 1, :] = face_in[...]
+    for n in range(steps):
+        low = weight[n, pl.ds(0, levels, stride=lat_rows), :]
+        high = weight[n, pl.ds(lat_rows - 1, levels, stride=lat_rows), :]
+        edge_gain[n, 0] = -jnp.minimum(face_in[n], 0.0) * low
+        edge_gain[n, 1] = jnp.maximum(faces[n, :, PAD + lat_rows - 1, :], 0.0) * high
+    for t in range(tracers):
+        add_flux(last, t)
+        lat_stencil(last, t)
+
+    for n in range(last, -1, -1):
+        rests = []
         for t in range(tracers):
-            for b in range(blocks):
-                rest_all[n, 0, t, b:b + 1, :] = rest[t][b * SUB:b * SUB + 1, :]
-        rest_copies = [
-            remote(rest_all.at[n, 0], rest_all.at[n, k], rest_send.at[n, k], rest_recv.at[n, k], lon_peer(k))
-            for k in range(1, n_lon)
-        ]
-        for copy in rest_copies:
-            copy.start()
-        if n == steps - 1:
+            wait_edges(n, t)
+            rests.append(block_rest(n, t))
+        if n == 0:
+            flux_copy.start()
+        if n == last:
             for copy in gain_copies:
                 copy.wait()
         whole = gain_all[0, n]
         for k in range(1, n_lon):
             whole = whole * gain_all[k, n]
-        for copy in rest_copies:
-            copy.wait()
-        ends = []
+        scale = 1.0 / (1.0 - whole)
         for t in range(tracers):
-            total = rest_all[n, 0, t]
-            for k in range(1, n_lon):
-                total = rest_all[n, k, t] + gain_all[k, n] * total
-            closure = total / (1.0 - whole)
-            wide = jnp.concatenate(
-                [jnp.broadcast_to(closure[b:b + 1, :], (SUB, LANES)) for b in range(blocks)], 0
-            )
-            inclusive = gain_levels[n, 3] * wide + rest[t]
-            end = jnp.where(sub == SUB - 1, wide, ahead(inclusive, 1))
-            ends.append(end.reshape(blocks, SUB, LANES))
-        for p in range(seg - 1, -1, -1):
-            r = gain_at(p)
-            for t in range(tracers):
-                ends[t] = r * ends[t] + rows_t[row_at(t, p)]
-                rows_t[row_at(t, p)] = ends[t]
-
-        target = rows if n > 0 else out_ref
-
-        def turn_back(b, carry):
-            target[pl.ds(pl.multiple_of(b * LANES, LANES), LANES), :] = rows_t[b].T
-            return carry
-
-        lax.fori_loop(0, tracers * blocks, turn_back, 0, unroll=4)
-
-        if n > 0:
-            def add(i, carry):
-                solved = rows[pl.ds(pl.multiple_of(i * lat_rows, SUB), lat_rows), :]
-                field[i, PAD:PAD + lat_rows, :] = solved + forcing[n - 1, i]
-                return carry
-
-            lax.fori_loop(0, fields, add, 0, unroll=2)
+            finish(n, t, rests[t], scale)
+            if n > 0:
+                next_field(n - 1, t)
+            else:
+                result_copy(t).start()
+    for t in range(tracers):
+        result_copy(t).wait()
+    flux_copy.wait()
 
 
 def shards(east_courant, north_courant, kernels, departures, cells, counts):
@@ -366,17 +431,22 @@
     dims = (steps, tracers, levels, lat_rows, n_lat, n_lon, slots, capacity)
     vmem = pltpu.VMEM
     dma = pltpu.SemaphoreType.DMA
-    whole = pl.BlockSpec(memory_space=pltpu.VMEM)
-    anywhere = pl.BlockSpec(memory_space=pl.ANY)
+    far = pl.BlockSpec(memory_space=pltpu.HBM)
     state, flux = pl.pallas_call(
         functools.partial(kernel, dims),
         out_shape=(
             jax.ShapeDtypeStruct((tracers * merged, lon_cells), F32),
             jax.ShapeDtypeStruct((tracers, lat_rows, lon_cells), F32),
         ),
-        in_specs=[anywhere, anywhere, whole, whole, whole, whole],
-        out_specs=(whole, whole),
+        in_specs=[far] * 6,
+        out_specs=(far, far),
         scratch_shapes=[
+            vmem((tracers, lat_rows, lon_cells), F32),
+            vmem(kernels.shape, F32),
+            vmem(departures.shape, F32),
+            vmem(cells.shape, jnp.int32),
+            vmem(counts.shape, jnp.int32),
+            vmem((steps, 2, levels, LANES), F32),
             vmem((steps, merged, LANES), F32),
             vmem((steps, levels, lat_rows + PAD, LANES), F32),
             vmem((steps, blocks, LANES, LANES), F32),
@@ -394,22 +464,22 @@
             vmem((fields, slots), F32),
             vmem((SUB * lat_rows // 2, 2 * slots), BF16),
             vmem((2 * slots, 2 * LANES), BF16),
-            vmem((steps, 2, fields, LANES), F32),
-            vmem((steps, 2, fields, LANES), F32),
+            vmem((steps, 2, tracers, levels, LANES), F32),
+            vmem((steps, 2, tracers, levels, LANES), F32),
             vmem((steps, levels, LANES), F32),
             vmem((steps, levels, LANES), F32),
             vmem((n_lon, steps, padded, LANES), F32),
-            vmem((steps, n_lon, tracers, padded, LANES), F32),
-            dma((2,)),
+            vmem((steps, tracers, n_lon, padded, LANES), F32),
+            dma((7 + tracers,)),
             dma((n_lon,)), dma((n_lon,)),
             dma((n_lat,)), dma((n_lat,)),
             dma((n_lon,)), dma((n_lon,)),
-            dma((steps, n_lon)), dma((steps, n_lon)),
-            dma((steps, 2)), dma((steps, 2)),
+            dma((steps, tracers, n_lon)), dma((steps, tracers, n_lon)),
+            dma((steps, 2, tracers)), dma((steps, 2, tracers)),
             dma((2,)),
         ],
         compiler_params=pltpu.CompilerParams(
-            collective_id=0, has_side_effects=True, vmem_limit_bytes=48 * 1024 * 1024
+            collective_id=0, has_side_effects=True, vmem_limit_bytes=60 * 1024 * 1024
         ),
         name="adjoint_window",
     )(

time: 44.8 us -> 38.2 us (0.85)
  local copies, waits for them, and re-layouts: 7.4 us -> 3.33 us
  Pallas kernels: 36.4 us -> 34.1 us
    unnamed x14 -> x4, local copies, waits for them, and re-layouts: 7.4 us -> 3.33 us
    pallas_call x1, Pallas kernels: 36.4 us -> 34.1 us  [shards(): pl.pallas_call(functools.partial(kernel, dims), out_shape=(jax.ShapeDtype...]
where the time goes in v2:
time: 38.2 us; the launch traced here: 38.1 us
  Pallas kernels  34.1 us (89%)
  local copies, waits for them, and re-layouts  3.33 us (9%)
  between operations  0.65 us (2%)
    pallas_call x1, Pallas kernels, shards(): pl.pallas_call(functools.partial(kernel, dims), out_shape=(jax.ShapeDtype...  34.1 us
    unnamed x4, local copies, waits for them, and re-layouts  3.33 us

profile of v2, /device:TPU:0, one launch (start us, length us, event | category | flops | bytes accessed | tf_op | source)
XLA Modules:
  0.0 38.1 jit_solution(17007838601124879132)
XLA Ops:
  0.6 34.1 %adjoint_window.1 = (f32[3072,128]{1,0:T(8,128)}, f32[2,96,128]{2,1,0:T(8,128)}) custom-call(f32[2,1536,128]{2,1,0:T(8,128)} %bitcast.2, f32[2,16,96,128]{3,2,1,0:T(8,128)} %north_hbm.1, f32[2,16,256]{2,1,0:T(8,128)} %kern_hbm.1, f32[2,2,256]{2,1,0:T(2,128)} %dep_hbm.1, s32[2,256]{1,0:T(2,128)} %cells_hbm.1, s32[2,32]{1,0:T(2,128)} %counts_hbm.1), custom_call_target="tpu_custom_call" | custom-call | tf_op jit(solution)/shard_map/adjoint_window/pallas_call | solution.py:435
  34.7 0.0 copy-start
  34.7 2.7 %copy.10 = f32[2,16,96,128]{3,2,1,0:T(8,128)} copy(f32[2,16,96,128]{3,2,1,0:T(8,128)} %bitcast.3) | data formatting | bytes 3145728
  37.4 0.0 copy-done
  37.4 0.6 %copy.11 = f32[2,96,128]{2,1,0:T(8,128)} copy(f32[2,96,128]{2,1,0:T(8,128)S(1)} %copy-done) | data formatting | bytes 196608
Async XLA Ops:
  34.7 2.7 %copy-start = (f32[2,96,128]{2,1,0:T(8,128)S(1)}, f32[2,96,128]{2,1,0:T(8,128)}, u32[]{:S(2)}) copy-start(f32[2,96,128]{2,1,0:T(8,128)} %get-tuple-element.9) | copy-start | bytes 294916

commit v3 on v2

--- a/solution.py
+++ b/solution.py
@@ -18,13 +18,12 @@
 def kernel(
     dims,
     east_hbm, north_hbm, kern_hbm, dep_hbm, cells_hbm, counts_hbm,
-    out_hbm, flux_hbm,
-    flux_ref,
+    out_ref, flux_ref,
     kern_ref, dep_ref, cells_ref, counts_ref, edge_gain,
-    weight, faces, gain_t, gain_levels, field, rows, rows_t, forcing,
-    features, sent, stage_lon, stage_lat, got_t, term_hi, term_lo, left, onehot,
+    weight, faces, turned, gain_seg, source_seg, gain_levels, field, rows, rows_t, forcing,
+    features, sent, stage, got_t, term_hi, term_lo, left, onehot,
     edge_out, edge_in, face_out, face_in, gain_all, rest_all,
-    local_sem, lon_send, lon_recv, lat_send, lat_recv, gain_send, gain_recv,
+    local_sem, slot_sem, gain_send, gain_recv,
     rest_send, rest_recv, edge_send, edge_recv, face_sem,
 ):
     steps, tracers, levels, lat_rows, n_lat, n_lon, slots, capacity = dims
@@ -37,11 +36,12 @@
     has_up = my_lat < n_lat - 1
     has_down = my_lat > 0
 
+    lat_ids = [lax.rem(my_lat + i, n_lat) for i in range(n_lat)]
+    lon_ids = [lax.rem(my_lon + j, n_lon) for j in range(n_lon)]
+    offsets = [(i, j) for i in range(n_lat) for j in range(n_lon)][1:]
+
     def lon_peer(k):
-        return (my_lat, lax.rem(my_lon + k, n_lon))
-
-    def lat_peer(k):
-        return (lax.rem(my_lat + k, n_lat), my_lon)
+        return (my_lat, lon_ids[k])
 
     def remote(src, dst, send, recv, device):
         return pltpu.make_async_remote_copy(
@@ -71,10 +71,10 @@
     field[:, PAD - 1, :] = jnp.zeros((fields, LANES), F32)
     field[:, PAD + lat_rows, :] = jnp.zeros((fields, LANES), F32)
     barrier = pltpu.get_barrier_semaphore()
-    for k in range(1, n_lon):
-        pl.semaphore_signal(barrier, inc=1, device_id=lon_peer(k), device_id_type=MESH)
-    for k in range(1, n_lat):
-        pl.semaphore_signal(barrier, inc=1, device_id=lat_peer(k), device_id_type=MESH)
+    for i, j in offsets:
+        pl.semaphore_signal(
+            barrier, inc=1, device_id=(lat_ids[i], lon_ids[j]), device_id_type=MESH
+        )
 
     for copy in small:
         copy.wait()
@@ -95,21 +95,15 @@
             at = dep_row + n * tracers + t
             features[at:at + 1, :] = dep_ref[n, t:t + 1, :] * live[n:n + 1, :]
         features[cell_row + n:cell_row + n + 1, :] = cells_ref[n:n + 1, :].astype(F32)
-    by_slot = features[...].T
-    for p in range(n_lat):
-        for q in range(n_lon):
-            at = (p * n_lon + q) * capacity
-            sent[q, p] = by_slot[at:at + capacity]
-    pl.semaphore_wait(barrier, n_lon - 1 + n_lat - 1)
-
-    lon_copies = [
-        remote(sent.at[lax.rem(my_lon + k, n_lon)], stage_lon.at[k],
-               lon_send.at[k], lon_recv.at[k], lon_peer(k))
-        for k in range(1, n_lon)
-    ]
-    for copy in lon_copies:
-        copy.start()
-    stage_lon[0] = sent[my_lon]
+    sent[...] = features[...].T.reshape(sent.shape)
+    pl.semaphore_wait(barrier, len(offsets))
+
+    for i, j in offsets:
+        remote(
+            sent.at[lat_ids[i] * n_lon + lon_ids[j]], stage.at[i * n_lon + j],
+            slot_sem.at[0], slot_sem.at[1], (lat_ids[i], lon_ids[j]),
+        ).start()
+    stage[0] = sent[my_lat * n_lon + my_lon]
 
     load_north.wait()
     face_out[...] = faces[:, :, PAD + lat_rows - 1, :]
@@ -139,14 +133,15 @@
             east = weight[n, at, :]
             share = 1.0 / (1.0 + east)
             weight[n, at, :] = share
-            gain_t[n, b] = (east * share).T
+            turned[b] = (east * share).T
             return carry
 
         lax.fori_loop(0, blocks, one, 0, unroll=2)
-        g = gain_t[n, :, pl.ds(seg - 1, SUB, stride=seg), :]
-        for p in range(seg - 2, -1, -1):
-            g = g * gain_t[n, :, pl.ds(p, SUB, stride=seg), :]
-        g = flat(g)
+        g = None
+        for p in range(seg - 1, -1, -1):
+            part = flat(turned[:, pl.ds(p, SUB, stride=seg), :])
+            gain_seg[n, p] = part
+            g = part if g is None else g * part
         for level, d in enumerate((1, 2, 4)):
             gain_levels[n, level] = g
             g = jnp.where(sub < SUB - d, g * ahead(g, d), g)
@@ -157,16 +152,6 @@
     load_east.wait()
     gains(steps - 1)
 
-    for copy in lon_copies:
-        copy.wait()
-    lat_copies = [
-        remote(stage_lon.at[:, lax.rem(my_lat + k, n_lat)], stage_lat.at[k],
-               lat_send.at[k], lat_recv.at[k], lat_peer(k))
-        for k in range(1, n_lat)
-    ]
-    for copy in lat_copies:
-        copy.start()
-    stage_lat[0] = stage_lon[:, my_lat]
     for n in range(steps - 2, -1, -1):
         gains(n)
     gain_copies = [
@@ -175,10 +160,10 @@
     ]
     for copy in gain_copies:
         copy.start()
-    for copy in lat_copies:
-        copy.wait()
-
-    got = stage_lat[...].reshape(slots, LANES)
+    arrived = stage.at[pl.ds(1, owners - 1)]
+    all_slots = remote(arrived, arrived, slot_sem.at[0], slot_sem.at[1], lon_peer(1))
+    all_slots.wait_recv()
+    got = stage[...].reshape(slots, LANES)
     got_t[...] = got.T
     group = SUB
     shift = LANES.bit_length() - 1
@@ -197,7 +182,7 @@
             term_lo[t * levels:(t + 1) * levels, :] = term - high
         lane_cell = got_t[cell_row + n:cell_row + n + 1, :].astype(jnp.int32)
         slot_row, _ = split_cell(lane_cell)
-        _, slot_col = split_cell(stage_lat[...].reshape(slots, LANES)[
+        _, slot_col = split_cell(stage[...].reshape(slots, LANES)[
             :, cell_row + n:cell_row + n + 1].astype(jnp.int32))
         hot = (
             lax.broadcasted_iota(jnp.int32, (slots, 2 * LANES), 1) == slot_col
@@ -292,9 +277,6 @@
 
         lax.fori_loop(0, levels, one, 0, unroll=2)
 
-    def gain_at(n, p):
-        return gain_t[n, :, pl.ds(p, SUB, stride=seg), :]
-
     def row_at(t, p):
         return (pl.ds(t * blocks, blocks), pl.ds(p, SUB, stride=seg), slice(None))
 
@@ -309,10 +291,11 @@
             return carry
 
         lax.fori_loop(0, blocks, turn, 0, unroll=4)
-        rest = rows_t[row_at(t, seg - 1)]
-        for p in range(seg - 2, -1, -1):
-            rest = gain_at(n, p) * rest + rows_t[row_at(t, p)]
-        rest = flat(rest)
+        rest = None
+        for p in range(seg - 1, -1, -1):
+            part = flat(rows_t[row_at(t, p)])
+            source_seg[t, p] = part
+            rest = part if rest is None else gain_seg[n, p] * rest + part
         for level, d in enumerate((1, 2, 4)):
             rest = jnp.where(sub < SUB - d, rest + gain_levels[n, level] * ahead(rest, d), rest)
         for b in range(blocks):
@@ -332,14 +315,15 @@
             [jnp.broadcast_to(closure[b:b + 1, :], (SUB, LANES)) for b in range(blocks)], 0
         )
         inclusive = gain_levels[n, 3] * wide + rest
-        end = jnp.where(sub == SUB - 1, wide, ahead(inclusive, 1)).reshape(blocks, SUB, LANES)
+        end = jnp.where(sub == SUB - 1, wide, ahead(inclusive, 1))
         for p in range(seg - 1, -1, -1):
-            end = gain_at(n, p) * end + rows_t[row_at(t, p)]
-            rows_t[row_at(t, p)] = end
+            end = gain_seg[n, p] * end + source_seg[t, p]
+            rows_t[row_at(t, p)] = end.reshape(blocks, SUB, LANES)
+        target = rows if n > 0 else out_ref
 
         def turn_back(b, carry):
             b = b + t * blocks
-            rows[pl.ds(pl.multiple_of(b * LANES, LANES), LANES), :] = rows_t[b].T
+            target[pl.ds(pl.multiple_of(b * LANES, LANES), LANES), :] = rows_t[b].T
             return carry
 
         lax.fori_loop(0, blocks, turn_back, 0, unroll=4)
@@ -360,11 +344,6 @@
         add_flux(n, t)
         lat_stencil(n, t)
 
-    def result_copy(t):
-        some = pl.ds(t * merged, merged)
-        return pltpu.make_async_copy(rows.at[some], out_hbm.at[some], local_sem.at[6 + t])
-
-    flux_copy = pltpu.make_async_copy(flux_ref, flux_hbm, local_sem.at[6 + tracers])
     last = steps - 1
     for t in range(tracers):
         some = slice(t * levels, (t + 1) * levels)
@@ -397,8 +376,6 @@
         for t in range(tracers):
             wait_edges(n, t)
             rests.append(block_rest(n, t))
-        if n == 0:
-            flux_copy.start()
         if n == last:
             for copy in gain_copies:
                 copy.wait()
@@ -410,11 +387,7 @@
             finish(n, t, rests[t], scale)
             if n > 0:
                 next_field(n - 1, t)
-            else:
-                result_copy(t).start()
-    for t in range(tracers):
-        result_copy(t).wait()
-    flux_copy.wait()
+    all_slots.wait_send()
 
 
 def shards(east_courant, north_courant, kernels, departures, cells, counts):
@@ -431,17 +404,17 @@
     dims = (steps, tracers, levels, lat_rows, n_lat, n_lon, slots, capacity)
     vmem = pltpu.VMEM
     dma = pltpu.SemaphoreType.DMA
+    near = pl.BlockSpec(memory_space=pltpu.VMEM)
     far = pl.BlockSpec(memory_space=pltpu.HBM)
     state, flux = pl.pallas_call(
         functools.partial(kernel, dims),
         out_shape=(
-            jax.ShapeDtypeStruct((tracers * merged, lon_cells), F32),
-            jax.ShapeDtypeStruct((tracers, lat_rows, lon_cells), F32),
+            vmem((tracers * merged, lon_cells), F32),
+            vmem((tracers, lat_rows, lon_cells), F32),
         ),
         in_specs=[far] * 6,
-        out_specs=(far, far),
+        out_specs=(near, near),
         scratch_shapes=[
-            vmem((tracers, lat_rows, lon_cells), F32),
             vmem(kernels.shape, F32),
             vmem(departures.shape, F32),
             vmem(cells.shape, jnp.int32),
@@ -449,16 +422,17 @@
             vmem((steps, 2, levels, LANES), F32),
             vmem((steps, merged, LANES), F32),
             vmem((steps, levels, lat_rows + PAD, LANES), F32),
-            vmem((steps, blocks, LANES, LANES), F32),
+            vmem((blocks, LANES, LANES), F32),
+            vmem((steps, LANES // SUB, blocks * SUB, LANES), F32),
+            vmem((tracers, LANES // SUB, blocks * SUB, LANES), F32),
             vmem((steps, 4, blocks * SUB, LANES), F32),
             vmem((fields, lat_rows + 2 * PAD, LANES), F32),
             vmem((tracers * merged, LANES), F32),
             vmem((tracers * blocks, LANES, LANES), F32),
             vmem((max(steps - 1, 1), fields, lat_rows, LANES), F32),
             vmem((LANES, slots), F32),
-            vmem((n_lon, n_lat, capacity, LANES), F32),
-            vmem((n_lon, n_lat, capacity, LANES), F32),
-            vmem((n_lat, n_lon, capacity, LANES), F32),
+            vmem((owners, capacity, LANES), F32),
+            vmem((owners, capacity, LANES), F32),
             vmem((LANES, slots), F32),
             vmem((fields, slots), F32),
             vmem((fields, slots), F32),
@@ -470,21 +444,25 @@
             vmem((steps, levels, LANES), F32),
             vmem((n_lon, steps, padded, LANES), F32),
             vmem((steps, tracers, n_lon, padded, LANES), F32),
-            dma((7 + tracers,)),
-            dma((n_lon,)), dma((n_lon,)),
-            dma((n_lat,)), dma((n_lat,)),
+            dma((6,)),
+            dma((2,)),
             dma((n_lon,)), dma((n_lon,)),
             dma((steps, tracers, n_lon)), dma((steps, tracers, n_lon)),
             dma((steps, 2, tracers)), dma((steps, 2, tracers)),
             dma((2,)),
         ],
         compiler_params=pltpu.CompilerParams(
-            collective_id=0, has_side_effects=True, vmem_limit_bytes=60 * 1024 * 1024
+            collective_id=0, has_side_effects=True, vmem_limit_bytes=40 * 1024 * 1024
         ),
         name="adjoint_window",
     )(
-        east_courant.reshape(steps, merged, lon_cells), north_courant,
-        kernels, departures, cells, counts,
+        *(
+            pltpu.with_memory_space_constraint(x, pltpu.HBM)
+            for x in (
+                east_courant.reshape(steps, merged, lon_cells), north_courant,
+                kernels, departures, cells, counts,
+            )
+        )
     )
     return state.reshape(tracers, levels, lat_rows, lon_cells), flux
 

time: 38.2 us -> 32.3 us (0.85)
  Pallas kernels: 34.1 us -> 29.8 us
  local copies, waits for them, and re-layouts: 3.33 us -> 1.79 us
    pallas_call x1, Pallas kernels: 34.1 us -> 29.8 us  [shards(): pl.pallas_call(functools.partial(kernel, dims), out_shape=(vmem((tracers...]
    unnamed x4 -> x2, local copies, waits for them, and re-layouts: 3.33 us -> 1.79 us
where the time goes in v3:
time: 32.3 us; the launch traced here: 32.2 us
  Pallas kernels  29.8 us (92%)
  local copies, waits for them, and re-layouts  1.79 us (6%)
  between operations  0.64 us (2%)
    pallas_call x1, Pallas kernels, shards(): pl.pallas_call(functools.partial(kernel, dims), out_shape=(vmem((tracers...  29.8 us
    unnamed x2, local copies, waits for them, and re-layouts  1.79 us

profile of v3, /device:TPU:0, one launch (start us, length us, event | category | flops | bytes accessed | tf_op | source)
XLA Modules:
  0.0 32.2 jit_solution(16266599946939737938)
XLA Ops:
  0.6 29.8 %adjoint_window.1 = (f32[3072,128]{1,0:T(8,128)S(1)}, f32[2,96,128]{2,1,0:T(8,128)S(1)}) custom-call(f32[2,1536,128]{2,1,0:T(8,128)} %bitcast.3, f32[2,16,96,128]{3,2,1,0:T(8,128)} %north_hbm.1, f32[2,16,256]{2,1,0:T(8,128)} %kern_hbm.1, f32[2,2,256]{2,1,0:T(2,128)} %dep_hbm.1, s32[2,256]{1,0:T(2,128)} %cells_hbm.1, s32[2,32]{1,0:T(2,128)} %counts_hbm.1), custom_call_target="tpu_custom_call" | custom-call | tf_op jit(solution)/shard_map/adjoint_window/pallas_call | solution.py:409
  30.4 1.1 %copy.10 = f32[2,16,96,128]{3,2,1,0:T(8,128)} copy(f32[2,16,96,128]{3,2,1,0:T(8,128)S(1)} %bitcast.2) | data formatting | bytes 3145728
  31.5 0.6 %copy.11 = f32[2,96,128]{2,1,0:T(8,128)} copy(f32[2,96,128]{2,1,0:T(8,128)S(1)} %get-tuple-element.7) | data formatting | bytes 196608

commit v4 on v3

--- a/solution.py
+++ b/solution.py
@@ -18,9 +18,9 @@
 def kernel(
     dims,
     east_hbm, north_hbm, kern_hbm, dep_hbm, cells_hbm, counts_hbm,
-    out_ref, flux_ref,
+    gain_seg, source_seg, end_ref, flux_ref,
     kern_ref, dep_ref, cells_ref, counts_ref, edge_gain,
-    weight, faces, turned, gain_seg, source_seg, gain_levels, field, rows, rows_t, forcing,
+    weight, faces, turned, gain_levels, field, rows, rows_t, forcing,
     features, sent, stage, got_t, term_hi, term_lo, left, onehot,
     edge_out, edge_in, face_out, face_in, gain_all, rest_all,
     local_sem, slot_sem, gain_send, gain_recv,
@@ -136,7 +136,7 @@
             turned[b] = (east * share).T
             return carry
 
-        lax.fori_loop(0, blocks, one, 0, unroll=2)
+        lax.fori_loop(0, blocks, one, 0, unroll=4)
         g = None
         for p in range(seg - 1, -1, -1):
             part = flat(turned[:, pl.ds(p, SUB, stride=seg), :])
@@ -147,18 +147,18 @@
             g = jnp.where(sub < SUB - d, g * ahead(g, d), g)
         gain_levels[n, 3] = g
         for b in range(blocks):
-            gain_all[0, n, b:b + 1, :] = g[b * SUB:b * SUB + 1, :]
+            gain_all[n, 0, b:b + 1, :] = g[b * SUB:b * SUB + 1, :]
 
     load_east.wait()
     gains(steps - 1)
 
-    for n in range(steps - 2, -1, -1):
-        gains(n)
-    gain_copies = [
-        remote(gain_all.at[0], gain_all.at[k], gain_send.at[k], gain_recv.at[k], lon_peer(k))
-        for k in range(1, n_lon)
-    ]
-    for copy in gain_copies:
+    def gain_copies(n):
+        return [
+            remote(gain_all.at[n, 0], gain_all.at[n, k], gain_send.at[n, k], gain_recv.at[n, k], lon_peer(k))
+            for k in range(1, n_lon)
+        ]
+
+    for copy in gain_copies(steps - 1):
         copy.start()
     arrived = stage.at[pl.ds(1, owners - 1)]
     all_slots = remote(arrived, arrived, slot_sem.at[0], slot_sem.at[1], lon_peer(1))
@@ -191,19 +191,16 @@
         onehot[slots:2 * slots, :] = hot
         here = lax.broadcasted_iota(jnp.int32, (half, slots), 0) == slot_row
 
-        def one(c, carry):
+        for c in range(fields // group):
             for i in range(group):
                 at = pl.ds(c * group + i, 1)
                 part = pl.ds(i * half, half)
-                left[part, 0:slots] = jnp.where(here, term_hi[at, :], 0.0).astype(BF16)
-                left[part, slots:2 * slots] = jnp.where(here, term_lo[at, :], 0.0).astype(BF16)
-            added = jnp.dot(left[...], onehot[...], preferred_element_type=F32)
+                left[c % 2, part, 0:slots] = jnp.where(here, term_hi[at, :], 0.0).astype(BF16)
+                left[c % 2, part, slots:2 * slots] = jnp.where(here, term_lo[at, :], 0.0).astype(BF16)
+            added = jnp.dot(left[c % 2], onehot[...], preferred_element_type=F32)
             for i in range(group):
                 block = added[i * half:(i + 1) * half]
                 store(c * group + i, block[:, :LANES], block[:, LANES:])
-            return carry
-
-        lax.fori_loop(0, fields // group, one, 0)
 
     def into_field(i, low, high):
         field[i, PAD:PAD + half, :] = low
@@ -290,7 +287,7 @@
             rows_t[b] = rows[pl.ds(pl.multiple_of(b * LANES, LANES), LANES), :].T
             return carry
 
-        lax.fori_loop(0, blocks, turn, 0, unroll=4)
+        lax.fori_loop(0, blocks, turn, 0, unroll=True)
         rest = None
         for p in range(seg - 1, -1, -1):
             part = flat(rows_t[row_at(t, p)])
@@ -309,24 +306,26 @@
             copy.wait()
         total = rest_all[n, t, 0]
         for k in range(1, n_lon):
-            total = rest_all[n, t, k] + gain_all[k, n] * total
+            total = rest_all[n, t, k] + gain_all[n, k] * total
         closure = total * scale
         wide = jnp.concatenate(
             [jnp.broadcast_to(closure[b:b + 1, :], (SUB, LANES)) for b in range(blocks)], 0
         )
         inclusive = gain_levels[n, 3] * wide + rest
         end = jnp.where(sub == SUB - 1, wide, ahead(inclusive, 1))
+        if n == 0:
+            end_ref[t] = end
+            return
         for p in range(seg - 1, -1, -1):
             end = gain_seg[n, p] * end + source_seg[t, p]
             rows_t[row_at(t, p)] = end.reshape(blocks, SUB, LANES)
-        target = rows if n > 0 else out_ref
 
         def turn_back(b, carry):
             b = b + t * blocks
-            target[pl.ds(pl.multiple_of(b * LANES, LANES), LANES), :] = rows_t[b].T
+            rows[pl.ds(pl.multiple_of(b * LANES, LANES), LANES), :] = rows_t[b].T
             return carry
 
-        lax.fori_loop(0, blocks, turn_back, 0, unroll=4)
+        lax.fori_loop(0, blocks, turn_back, 0, unroll=True)
 
     def next_field(n, t):
         some = slice(t * levels, (t + 1) * levels)
@@ -351,7 +350,9 @@
         edge_out[last, 1, t] = field[some, PAD + lat_rows - 1, :]
         send_edges(last, t)
     for m in range(steps - 2, -1, -1):
-        deposit(m, into_forcing(m))
+        gains(m)
+        for copy in gain_copies(m):
+            copy.start()
 
     @pl.when(has_down)
     def _():
@@ -377,17 +378,43 @@
             wait_edges(n, t)
             rests.append(block_rest(n, t))
         if n == last:
-            for copy in gain_copies:
-                copy.wait()
-        whole = gain_all[0, n]
+            for m in range(steps - 2, -1, -1):
+                deposit(m, into_forcing(m))
+        for copy in gain_copies(n):
+            copy.wait()
+        whole = gain_all[n, 0]
         for k in range(1, n_lon):
-            whole = whole * gain_all[k, n]
+            whole = whole * gain_all[n, k]
         scale = 1.0 / (1.0 - whole)
         for t in range(tracers):
             finish(n, t, rests[t], scale)
             if n > 0:
                 next_field(n - 1, t)
     all_slots.wait_send()
+
+
+def closing(
+    dims, gain_seg, source_seg, end_ref, flux_ref, out_hbm, flux_hbm, rows_t, rows, sems
+):
+    tracers, blocks, group = dims
+    seg = LANES // SUB
+    flux_copy = pltpu.make_async_copy(flux_ref, flux_hbm, sems.at[0])
+    flux_copy.start()
+    copies = [flux_copy]
+    for t in range(tracers):
+        end = end_ref[t]
+        for p in range(seg - 1, -1, -1):
+            end = gain_seg[0, p] * end + source_seg[t, p]
+            rows_t[t, :, pl.ds(p, SUB, stride=seg), :] = end.reshape(blocks, SUB, LANES)
+        for first in range(0, blocks, group):
+            for b in range(first, first + group):
+                at = (t * blocks + b) * LANES
+                rows[at:at + LANES, :] = rows_t[t, b].T
+            some = pl.ds((t * blocks + first) * LANES, group * LANES)
+            copies.append(pltpu.make_async_copy(rows.at[some], out_hbm.at[some], sems.at[len(copies)]))
+            copies[-1].start()
+    for copy in copies:
+        copy.wait()
 
 
 def shards(east_courant, north_courant, kernels, departures, cells, counts):
@@ -406,14 +433,17 @@
     dma = pltpu.SemaphoreType.DMA
     near = pl.BlockSpec(memory_space=pltpu.VMEM)
     far = pl.BlockSpec(memory_space=pltpu.HBM)
-    state, flux = pl.pallas_call(
+    seg = LANES // SUB
+    parts = pl.pallas_call(
         functools.partial(kernel, dims),
         out_shape=(
-            vmem((tracers * merged, lon_cells), F32),
+            vmem((steps, seg, blocks * SUB, LANES), F32),
+            vmem((tracers, seg, blocks * SUB, LANES), F32),
+            vmem((tracers, blocks * SUB, LANES), F32),
             vmem((tracers, lat_rows, lon_cells), F32),
         ),
         in_specs=[far] * 6,
-        out_specs=(near, near),
+        out_specs=(near,) * 4,
         scratch_shapes=[
             vmem(kernels.shape, F32),
             vmem(departures.shape, F32),
@@ -423,8 +453,6 @@
             vmem((steps, merged, LANES), F32),
             vmem((steps, levels, lat_rows + PAD, LANES), F32),
             vmem((blocks, LANES, LANES), F32),
-            vmem((steps, LANES // SUB, blocks * SUB, LANES), F32),
-            vmem((tracers, LANES // SUB, blocks * SUB, LANES), F32),
             vmem((steps, 4, blocks * SUB, LANES), F32),
             vmem((fields, lat_rows + 2 * PAD, LANES), F32),
             vmem((tracers * merged, LANES), F32),
@@ -436,17 +464,17 @@
             vmem((LANES, slots), F32),
             vmem((fields, slots), F32),
             vmem((fields, slots), F32),
-            vmem((SUB * lat_rows // 2, 2 * slots), BF16),
+            vmem((2, SUB * lat_rows // 2, 2 * slots), BF16),
             vmem((2 * slots, 2 * LANES), BF16),
             vmem((steps, 2, tracers, levels, LANES), F32),
             vmem((steps, 2, tracers, levels, LANES), F32),
             vmem((steps, levels, LANES), F32),
             vmem((steps, levels, LANES), F32),
-            vmem((n_lon, steps, padded, LANES), F32),
+            vmem((steps, n_lon, padded, LANES), F32),
             vmem((steps, tracers, n_lon, padded, LANES), F32),
             dma((6,)),
             dma((2,)),
-            dma((n_lon,)), dma((n_lon,)),
+            dma((steps, n_lon)), dma((steps, n_lon)),
             dma((steps, tracers, n_lon)), dma((steps, tracers, n_lon)),
             dma((steps, 2, tracers)), dma((steps, 2, tracers)),
             dma((2,)),
@@ -464,6 +492,23 @@
             )
         )
     )
+    group = 4 if blocks % 4 == 0 else 1
+    state, flux = pl.pallas_call(
+        functools.partial(closing, (tracers, blocks, group)),
+        out_shape=(
+            jax.ShapeDtypeStruct((tracers * merged, lon_cells), F32),
+            jax.ShapeDtypeStruct((tracers, lat_rows, lon_cells), F32),
+        ),
+        in_specs=[near] * 4,
+        out_specs=(pl.BlockSpec(memory_space=pl.ANY),) * 2,
+        scratch_shapes=[
+            vmem((tracers, blocks, LANES, LANES), F32),
+            vmem((tracers * merged, LANES), F32),
+            dma((1 + tracers * (blocks // group),)),
+        ],
+        compiler_params=pltpu.CompilerParams(vmem_limit_bytes=16 * 1024 * 1024),
+        name="closing",
+    )(*parts)
     return state.reshape(tracers, levels, lat_rows, lon_cells), flux
 
 

time: 32.3 us -> 29.7 us (0.920)
  local copies, waits for them, and re-layouts: 1.79 us -> 0 us
  Pallas kernels: 29.8 us -> 28.9 us
    unnamed x2 -> x0, local copies, waits for them, and re-layouts: 1.79 us -> none
    pallas_call x1 -> x2, Pallas kernels: 29.8 us -> 28.9 us  [the longest x1 27.3 us: shards(): pl.pallas_call(functools.partial(kernel, dims), out_shape=(vmem((steps, s...]
where the time goes in v4:
time: 29.7 us; the launch traced here: 29.6 us
  Pallas kernels  28.9 us (97%)
  between operations  0.64 us (2%)
    pallas_call x1, Pallas kernels, shards(): pl.pallas_call(functools.partial(kernel, dims), out_shape=(vmem((steps, s...  27.3 us
    pallas_call x1, Pallas kernels, shards(): pl.pallas_call(functools.partial(closing, (tracers, blocks, group)), out_...  1.57 us

profile of v4, /device:TPU:0, one launch (start us, length us, event | category | flops | bytes accessed | tf_op | source)
XLA Modules:
  0.0 29.6 jit_solution(13660106632997098569)
XLA Ops:
  0.6 27.3 %adjoint_window.1 = (f32[2,16,96,128]{3,2,1,0:T(8,128)S(1)}, f32[2,16,96,128]{3,2,1,0:T(8,128)S(1)}, f32[2,96,128]{2,1,0:T(8,128)S(1)}, f32[2,96,128]{2,1,0:T(8,128)S(1)}) custom-call(f32[2,1536,128]{2,1,0:T(8,128)} %bitcast.2, f32[2,16,96,128]{3,2,1,0:T(8,128)} %north_hbm.1, f32[2,16,256]{2,1,0:T(8,128)} %kern_hbm.1, f32[2,2,256]{2,1,0:T(2,128)} %dep_hbm.1, ...), custom_call_target="tpu_custom_call" | custom-call | tf_op jit(solution)/shard_map/adjoint_window/pallas_call | solution.py:437
  28.0 1.6 %closing.1 = (f32[3072,128]{1,0:T(8,128)}, f32[2,96,128]{2,1,0:T(8,128)}) custom-call(f32[2,16,96,128]{3,2,1,0:T(8,128)S(1)} %get-tuple-element.8.gain_seg, f32[2,16,96,128]{3,2,1,0:T(8,128)S(1)} %get-tuple-element.9.source_seg, f32[2,96,128]{2,1,0:T(8,128)S(1)} %get-tuple-element.10.end_ref, f32[2,96,128]{2,1,0:T(8,128)S(1)} %get-tuple-element.11.flux_ref), custom_call_target="tpu_custom_call" | custom-call | tf_op jit(solution)/shard_map/closing/pallas_call | solution.py:496

commit v5 on v4

--- a/solution.py
+++ b/solution.py
@@ -166,6 +166,7 @@
     got = stage[...].reshape(slots, LANES)
     got_t[...] = got.T
     group = SUB
+    tile = 16
     shift = LANES.bit_length() - 1
 
     def split_cell(cell):
@@ -189,14 +190,20 @@
         ).astype(F32).astype(BF16)
         onehot[0:slots, :] = hot
         onehot[slots:2 * slots, :] = hot
-        here = lax.broadcasted_iota(jnp.int32, (half, slots), 0) == slot_row
+        here = (
+            lax.broadcasted_iota(jnp.int32, (half, slots), 0) == slot_row
+        ).astype(F32).astype(BF16).reshape(half // tile, tile, slots)
+
+        def placed(term):
+            wide = jnp.broadcast_to(term, (tile, slots)).astype(BF16)
+            return (here * wide[None]).reshape(half, slots)
 
         for c in range(fields // group):
             for i in range(group):
                 at = pl.ds(c * group + i, 1)
                 part = pl.ds(i * half, half)
-                left[c % 2, part, 0:slots] = jnp.where(here, term_hi[at, :], 0.0).astype(BF16)
-                left[c % 2, part, slots:2 * slots] = jnp.where(here, term_lo[at, :], 0.0).astype(BF16)
+                left[c % 2, part, 0:slots] = placed(term_hi[at, :])
+                left[c % 2, part, slots:2 * slots] = placed(term_lo[at, :])
             added = jnp.dot(left[c % 2], onehot[...], preferred_element_type=F32)
             for i in range(group):
                 block = added[i * half:(i + 1) * half]
@@ -272,7 +279,7 @@
             rows[pl.ds(pl.multiple_of(i * lat_rows, SUB), lat_rows), :] = share * y
             return carry
 
-        lax.fori_loop(0, levels, one, 0, unroll=2)
+        lax.fori_loop(0, levels, one, 0, unroll=4)
 
     def row_at(t, p):
         return (pl.ds(t * blocks, blocks), pl.ds(p, SUB, stride=seg), slice(None))
@@ -339,7 +346,7 @@
             field[i, PAD:PAD + lat_rows, :] = solved + forcing[n, i]
             return carry
 
-        lax.fori_loop(0, levels, add, 0, unroll=2)
+        lax.fori_loop(0, levels, add, 0, unroll=4)
         add_flux(n, t)
         lat_stencil(n, t)
 

time: 29.7 us -> 29.6 us (level)
  no operation moved by 1% of the time
where the time goes in v5:
time: 29.6 us; the launch traced here: 29.4 us
  Pallas kernels  28.8 us (97%)
  between operations  0.64 us (2%)
    pallas_call x1, Pallas kernels, shards(): pl.pallas_call(functools.partial(kernel, dims), out_shape=(vmem((steps, s...  27.2 us
    pallas_call x1, Pallas kernels, shards(): pl.pallas_call(functools.partial(closing, (tracers, blocks, group)), out_...  1.57 us

profile of v5, /device:TPU:0, one launch (start us, length us, event | category | flops | bytes accessed | tf_op | source)
XLA Modules:
  0.0 29.4 jit_solution(7245379274223919208)
XLA Ops:
  0.6 27.2 %adjoint_window.1 = (f32[2,16,96,128]{3,2,1,0:T(8,128)S(1)}, f32[2,16,96,128]{3,2,1,0:T(8,128)S(1)}, f32[2,96,128]{2,1,0:T(8,128)S(1)}, f32[2,96,128]{2,1,0:T(8,128)S(1)}) custom-call(f32[2,1536,128]{2,1,0:T(8,128)} %bitcast.2, f32[2,16,96,128]{3,2,1,0:T(8,128)} %north_hbm.1, f32[2,16,256]{2,1,0:T(8,128)} %kern_hbm.1, f32[2,2,256]{2,1,0:T(2,128)} %dep_hbm.1, ...), custom_call_target="tpu_custom_call" | custom-call | tf_op jit(solution)/shard_map/adjoint_window/pallas_call | solution.py:444
  27.9 1.6 %closing.1 = (f32[3072,128]{1,0:T(8,128)}, f32[2,96,128]{2,1,0:T(8,128)}) custom-call(f32[2,16,96,128]{3,2,1,0:T(8,128)S(1)} %get-tuple-element.8.gain_seg, f32[2,16,96,128]{3,2,1,0:T(8,128)S(1)} %get-tuple-element.9.source_seg, f32[2,96,128]{2,1,0:T(8,128)S(1)} %get-tuple-element.10.end_ref, f32[2,96,128]{2,1,0:T(8,128)S(1)} %get-tuple-element.11.flux_ref), custom_call_target="tpu_custom_call" | custom-call | tf_op jit(solution)/shard_map/closing/pallas_call | solution.py:503

commit v6 on v5

--- a/solution.py
+++ b/solution.py
@@ -160,6 +160,10 @@
 
     for copy in gain_copies(steps - 1):
         copy.start()
+    for m in range(steps - 2, -1, -1):
+        gains(m)
+        for copy in gain_copies(m):
+            copy.start()
     arrived = stage.at[pl.ds(1, owners - 1)]
     all_slots = remote(arrived, arrived, slot_sem.at[0], slot_sem.at[1], lon_peer(1))
     all_slots.wait_recv()
@@ -356,11 +360,6 @@
         edge_out[last, 0, t] = field[some, PAD, :]
         edge_out[last, 1, t] = field[some, PAD + lat_rows - 1, :]
         send_edges(last, t)
-    for m in range(steps - 2, -1, -1):
-        gains(m)
-        for copy in gain_copies(m):
-            copy.start()
-
     @pl.when(has_down)
     def _():
         face_copy.wait_recv()

time: 29.6 us -> 29.6 us (level)
  no operation moved by 1% of the time
where the time goes in v6:
time: 29.6 us; the launch traced here: 29.4 us
  Pallas kernels  28.8 us (97%)
  between operations  0.64 us (2%)
    pallas_call x1, Pallas kernels, shards(): pl.pallas_call(functools.partial(kernel, dims), out_shape=(vmem((steps, s...  27.2 us
    pallas_call x1, Pallas kernels, shards(): pl.pallas_call(functools.partial(closing, (tracers, blocks, group)), out_...  1.57 us

profile of v6, /device:TPU:0, one launch (start us, length us, event | category | flops | bytes accessed | tf_op | source)
XLA Modules:
  0.0 29.4 jit_solution(8495584185621121561)
XLA Ops:
  0.6 27.2 %adjoint_window.1 = (f32[2,16,96,128]{3,2,1,0:T(8,128)S(1)}, f32[2,16,96,128]{3,2,1,0:T(8,128)S(1)}, f32[2,96,128]{2,1,0:T(8,128)S(1)}, f32[2,96,128]{2,1,0:T(8,128)S(1)}) custom-call(f32[2,1536,128]{2,1,0:T(8,128)} %bitcast.2, f32[2,16,96,128]{3,2,1,0:T(8,128)} %north_hbm.1, f32[2,16,256]{2,1,0:T(8,128)} %kern_hbm.1, f32[2,2,256]{2,1,0:T(2,128)} %dep_hbm.1, ...), custom_call_target="tpu_custom_call" | custom-call | tf_op jit(solution)/shard_map/adjoint_window/pallas_call | solution.py:443
  27.9 1.6 %closing.1 = (f32[3072,128]{1,0:T(8,128)}, f32[2,96,128]{2,1,0:T(8,128)}) custom-call(f32[2,16,96,128]{3,2,1,0:T(8,128)S(1)} %get-tuple-element.8.gain_seg, f32[2,16,96,128]{3,2,1,0:T(8,128)S(1)} %get-tuple-element.9.source_seg, f32[2,96,128]{2,1,0:T(8,128)S(1)} %get-tuple-element.10.end_ref, f32[2,96,128]{2,1,0:T(8,128)S(1)} %get-tuple-element.11.flux_ref), custom_call_target="tpu_custom_call" | custom-call | tf_op jit(solution)/shard_map/closing/pallas_call | solution.py:502
